TPU v7x, 256 devices: a whole 4x4x8 slice. The times are simulated.
256 devices in a mesh: src: 32 (over y, z_hi, x), freq: 8 (over z_lo, core).
Axes of the slice: x: 4, y: 4, z: 8 (z_hi: 2, z_lo: 4; z = z_hi * 4 + z_lo), core: 2. Of those that a mesh axis runs over, the one named last changes fastest.
Arguments:
- source_dirs: float32 [2, 16384], P(None, 'src'), may hold values from -0.6 to 0.6
- flux: float32 [16384], P('src'), may hold values from 0.1 to 10
- beam: float32 [256, 16384], P('freq', 'src'), may hold values from 0.3 to 1
- counts: int32 [32], replicated, may hold values from 1 to 512, 8192 in all
- antennas: float32 [3, 128], replicated, may hold values from -30 to 30
- pairs: int32 [2, 4096], replicated, may hold values from 0 to 127, as said below
- data: float32 [2, 256, 4096], P(None, None, ('src', 'freq')), may hold values from -6 to 6
- delay_weight: float32 [256], replicated, may hold values from 0.3 to 3
Outputs:
- flux_grad: float32 [16384], P('src')
- beam_grad: float32 [256, 16384], P('freq', 'src')
Inputs may be any that keep to these rules, and one draw needn't show every extreme that they name: Live sources fill the first slots of each block; the counts sum to 8192 and the largest is exactly 512. `pairs`: each baseline names two different antennas.
All inputs are finite; a program needn't handle non-finite values.
Results may differ from a plain program's by a relative error of at most 0.0003.
Values sent between devices are 32-bit elements; how exact they have to be, the bound alone decides.
A program may use at most 128 MiB of HBM per device.

v0:
```python
import math

import jax
import jax.numpy as jnp
from jax import lax
from jax.sharding import PartitionSpec as P

NCH = 256


TWO_PI = 2.0 * math.pi
PRECISE = lax.Precision.HIGHEST


def precise_dot(left, right):
    return jnp.dot(left, right, precision=PRECISE, preferred_element_type=jnp.float32)


def channel_freqs(chan_index):
    return 1.0 + 0.6 * chan_index.astype(jnp.float32) / NCH


def phase_matrix(dir_block, antennas, chan_freqs):
    along_l = dir_block[0]
    along_m = dir_block[1]
    along_n = jnp.sqrt(1.0 - along_l * along_l - along_m * along_m)
    delay = (
        antennas[0][:, None] * along_l[None, :]
        + antennas[1][:, None] * along_m[None, :]
        + antennas[2][:, None] * along_n[None, :]
    )
    phase = (TWO_PI * chan_freqs)[:, None, None] * delay[None, :, :]
    return jnp.concatenate([jnp.cos(phase), jnp.sin(phase)], axis=1)


def gram_of(phased, weights):
    return jnp.einsum(
        "cas,cbs->cab",
        phased * weights[:, None, :],
        phased,
        precision=PRECISE,
        preferred_element_type=jnp.float32,
    )


def baseline_values(inner_product_matrix, pairs):
    antenna_left = pairs[0]
    antenna_right = pairs[1]
    antenna_total = inner_product_matrix.shape[1] // 2
    real_component = (
        inner_product_matrix[:, antenna_left, antenna_right]
        + inner_product_matrix[:, antenna_left + antenna_total, antenna_right + antenna_total]
    )
    imaginary_component = (
        inner_product_matrix[:, antenna_left + antenna_total, antenna_right]
        - inner_product_matrix[:, antenna_left, antenna_right + antenna_total]
    )
    return jnp.stack([real_component, imaginary_component])


def delay_tables():
    chan_index = jnp.arange(NCH, dtype=jnp.int32)
    turn_count = chan_index[:, None] * chan_index[None, :] % NCH
    angles = TWO_PI * turn_count.astype(jnp.float32) / NCH
    table_scale = 1.0 / math.sqrt(NCH)
    window_taper = 0.6 - 0.4 * jnp.cos(TWO_PI * (chan_index.astype(jnp.float32) + 0.5) / NCH)
    return (jnp.cos(angles) * table_scale, -jnp.sin(angles) * table_scale, window_taper)


def spectral_cotangent(visibility, data, delay_weight):
    cos_table, sin_table, window_taper = delay_tables()
    tapered_re = window_taper[:, None] * visibility[0]
    tapered_im = window_taper[:, None] * visibility[1]
    spec_re = precise_dot(cos_table, tapered_re) - precise_dot(sin_table, tapered_im)
    spec_im = precise_dot(cos_table, tapered_im) + precise_dot(sin_table, tapered_re)
    grad_re = delay_weight[:, None] * (spec_re - data[0])
    grad_im = delay_weight[:, None] * (spec_im - data[1])
    back_re = precise_dot(cos_table.T, grad_re) + precise_dot(sin_table.T, grad_im)
    back_im = precise_dot(cos_table.T, grad_im) - precise_dot(sin_table.T, grad_re)
    return jnp.stack([window_taper[:, None] * back_re, window_taper[:, None] * back_im])


def transpose_solver(upstream_gradient, pairs, antenna_total):
    channel_total = upstream_gradient.shape[1]
    blank_canvas = jnp.zeros((channel_total, antenna_total, antenna_total), jnp.float32)
    cot_real = blank_canvas.at[:, pairs[0], pairs[1]].add(upstream_gradient[0])
    cot_imag = blank_canvas.at[:, pairs[0], pairs[1]].add(upstream_gradient[1])
    upper_rows = jnp.concatenate([cot_real, -cot_imag], axis=2)
    lower_rows = jnp.concatenate([cot_imag, cot_real], axis=2)
    return jnp.concatenate([upper_rows, lower_rows], axis=1)


def weight_grads(kernel, phased):
    product = jnp.einsum(
        "cab,cbs->cas", kernel, phased, precision=PRECISE, preferred_element_type=jnp.float32
    )
    return jnp.sum(phased * product, axis=1)


def body(source_dirs, flux, beam, counts, antennas, pairs, data, delay_weight):
    src_count = lax.axis_size("src")
    src_rank = lax.axis_index("src")
    own_chans = beam.shape[0]
    own_slots = flux.shape[0]
    chan_first = lax.axis_index("freq") * own_chans
    chan_freqs = channel_freqs(chan_first + jnp.arange(own_chans, dtype=jnp.int32))
    flux_norm = 1.0 / math.sqrt(own_slots * src_count)
    slot_index = jnp.arange(own_slots, dtype=jnp.int32)
    live_mask = (slot_index < counts[src_rank]).astype(jnp.float32)
    live_scale = live_mask * flux_norm
    weights = flux[None, :] * beam * beam * live_scale[None, :]
    phased = phase_matrix(source_dirs, antennas, chan_freqs)
    partial_vis = baseline_values(gram_of(phased, weights), pairs)
    shares = lax.psum_scatter(partial_vis, "src", scatter_dimension=2, tiled=True)
    spectra = lax.all_to_all(shares, "freq", split_axis=2, concat_axis=1, tiled=True)
    upstream_gradient = spectral_cotangent(spectra, data, delay_weight)
    returned = lax.all_to_all(upstream_gradient, "freq", split_axis=1, concat_axis=2, tiled=True)
    full_cot = lax.all_gather(returned, "src", axis=2, tiled=True)
    kernel = transpose_solver(full_cot, pairs, antennas.shape[1])
    work_grads = weight_grads(kernel, phased)
    chan_sums = jnp.sum(work_grads * beam * beam, axis=0)
    flux_grad = lax.psum(chan_sums, "freq") * live_scale
    beam_grad = work_grads * (2.0 * flux * live_scale)[None, :] * beam
    return (flux_grad, beam_grad)


def solution(mesh):
    in_specs = (
        P(None, "src"),
        P("src"),
        P("freq", "src"),
        P(),
        P(),
        P(),
        P(None, None, ("src", "freq")),
        P(),
    )
    out_specs = (P("src"), P("freq", "src"))
    return jax.shard_map(body, mesh=mesh, in_specs=in_specs, out_specs=out_specs, check_vma=False)
```

profile of v0, /device:TPU:1, one launch (start us, length us, event | category | flops | bytes accessed | tf_op | source)
XLA Modules:
  0.0 1029.1 jit_solution(14409201809813471584)
XLA Ops:
  7.2 0.8 fusion.109
  8.0 0.8 slice_bitcast_fusion.6
  9.0 31.6 %multiply_cosine_fusion = (f32[32,128,512]{2,1,0:T(8,128)}, f32[32,128,512]{2,1,0:T(8,128)}) fusion(f32[128,512]{1,0:T(8,128)S(1)} %multiply_add_fusion, f32[32]{0:T(128)S(1)} %add_multiply_fusion), kind=kLoop, calls=%fused_computation.11 | loop fusion | flops 2097152 | bytes 17039488 | tf_op jit(solution)/shard_map/cos | solution.py:33
  40.6 0.7 dynamic_slice.3
  41.3 0.7 multiply_multiply_fusion.3
  42.0 26.4 %fusion = f32[32,256,256]{2,1,0:T(8,128)} fusion(f32[32,128,512]{2,1,0:T(8,128)} %get-tuple-element.6, f32[32,128,512]{2,1,0:T(8,128)} %get-tuple-element.5, f32[32,512]{1,0:T(8,128)S(1)} %fusion.40), kind=kOutput, calls=%fused_computation.6 | convolution fusion | flops 12897484800 | bytes 25231360 | tf_op jit(solution)/shard_map/cas,cbs->cab/dot_general | solution.py:37
  68.4 19.8 %copy.50 = f32[32,256,256]{0,2,1:T(8,128)} copy(f32[32,256,256]{2,1,0:T(8,128)} %fusion) | data formatting | bytes 16777216 | tf_op jit(solution)/shard_map/cas,cbs->cab/dot_general | solution.py:37
  88.4 40.4 %gather_fusion.3 = f32[4096,32]{1,0:T(8,128)S(1)} fusion(f32[32,256,256]{0,2,1:T(8,128)} %copy.50, s32[4096]{0:T(1024)S(1)} %bitcast.103), kind=kCustom, calls=%fused_computation.3 | custom fusion | bytes 1081344 | tf_op jit(solution)/shard_map/gather | solution.py:56
  128.8 59.5 %gather_fusion.2 = f32[4096,32]{1,0:T(8,128)} fusion(f32[32,256,256]{0,2,1:T(8,128)} %copy.50, s32[4096]{0:T(1024)S(1)} %bitcast.102), kind=kCustom, calls=%fused_computation.2 | custom fusion | bytes 1081344 | tf_op jit(solution)/shard_map/gather | solution.py:55
  188.3 59.6 %gather_fusion = f32[4096,32]{1,0:T(8,128)} fusion(f32[32,256,256]{0,2,1:T(8,128)} %copy.50, s32[4096]{0:T(1024)S(1)} %bitcast.101), kind=kCustom, calls=%fused_computation | custom fusion | bytes 1081344 | tf_op jit(solution)/shard_map/gather | solution.py:51
  247.9 59.4 %gather_fusion.1 = f32[4096,32]{1,0:T(8,128)} fusion(f32[32,256,256]{0,2,1:T(8,128)} %copy.50, s32[4096]{0:T(1024)S(1)} %bitcast.100), kind=kCustom, calls=%fused_computation.1 | custom fusion | bytes 1081344 | tf_op jit(solution)/shard_map/gather | solution.py:52
  307.3 2.0 subtract_bitcast_fusion
  309.3 0.3 copy-done
  309.5 0.6 copy-done.1
  310.4 0.3 pad_maximum_fusion.3
  310.7 16.6 %copy.54 = f32[2,32,4096]{1,0,2:T(2,128)} copy(f32[2,32,4096]{1,2,0:T(8,128)S(1)} %pad_maximum_fusion.3) | data formatting | bytes 2097152 | tf_op jit(solution)/shard_map/stack | solution.py:58
  327.3 0.6 copy-done.9
  327.9 0.6 dynamic-slice
  329.2 429.7 %all-reduce.3.cloned.1.call-done = f32[2,32,4096]{1,0,2:T(2,128)} async-done(((f32[2,32,4096]{1,0,2:T(2,128)}), f32[2,32,4096]{1,0,2:T(2,128)}) %all-reduce.3.cloned.1.call-update) | async-done | bytes 1048592
  758.8 0.9 fusion.110
  759.8 0.8 reshape.337
  760.5 25.4 %all-to-all-start = ((f32[8,1,1024]{2,1,0:T(1,128)}), f32[8,1,1024]{2,1,0:T(1,128)S(1)}, u32[]{:S(2)}, u32[]{:S(2)}) async-start(f32[8,1,1024]{2,1,0:T(1,128)} %reshape.337), calls=%async_computation | async-start | bytes 65536 | tf_op jit(solution)/shard_map/all_to_all | solution.py:115
  786.0 4.9 all-to-all-done
  790.9 0.5 broadcast.404
  791.4 0.7 reduce.6
  792.6 1.2 fusion.31
  793.8 1.3 fusion.29
  795.2 1.3 fusion.21
  796.5 1.2 fusion.30
  797.7 1.3 fusion.19
  799.0 1.2 fusion.28
  800.3 1.2 fusion.17
  801.5 1.2 fusion.15
  802.9 0.3 reshape.339
  803.3 8.3 all_to_all.33
  811.5 0.7 reduce.7
  812.3 0.4 reshape.340
  812.7 0.8 copy.57
  813.7 105.4 %all-gather.2.cloned.1.call-done = f32[2,32,4096]{1,2,0:T(8,128)} async-done(((f32[2,32,128]{1,2,0:T(8,128)}), f32[2,32,4096]{1,2,0:T(8,128)}) %all-gather.2.cloned.1.call-update) | async-done | bytes 1048592 | tf_op jit(solution)/shard_map/all_gather | solution.py:118
  919.0 24.4 %scatter_custom_fusion.1 = f32[32,16384]{0,1:T(8,128)} fusion(s32[4096]{0:T(1024)S(1)} %broadcast_select_fusion, f32[]{:T(128)} %constant.25.clone.1, f32[2,32,4096]{1,2,0:T(8,128)} %all-gather.2.cloned.1.call-done), kind=kCustom, calls=%fused_computation.21 | custom fusion | flops 131072 | bytes 4194816
  943.4 5.5 copy.61
  949.0 1.5 neg.13
  950.5 24.6 %scatter_custom_fusion = f32[32,16384]{0,1:T(8,128)} fusion(s32[4096]{0:T(1024)S(1)} %broadcast_select_fusion, f32[]{:T(128)} %constant.25.clone.1, f32[2,32,4096]{1,2,0:T(8,128)} %all-gather.2.cloned.1.call-done), kind=kCustom, calls=%fused_computation.23 | custom fusion | flops 131072 | bytes 4194816
  975.1 6.5 copy.60
  981.5 20.5 %multiply_reduce_fusion = f32[32,512]{1,0:T(8,128)S(1)} fusion(f32[32,128,512]{2,1,0:T(8,128)} %get-tuple-element.6, f32[32,128,512]{2,1,0:T(8,128)} %get-tuple-element.5, f32[32,128,128]{2,1,0:T(8,128)} %copy.60, f32[32,128,128]{2,1,0:T(8,128)S(1)} %copy.61, f32[32,128,128]{2,1,0:T(8,128)} %neg.13), kind=kOutput, calls=%fused_computation.9 | convolution fusion | flops 12903759872 | bytes 23134208 | tf_op jit(solution)/shard_map/cab,cbs->cas/dot_general | solution.py:94
  1002.1 0.6 multiply_multiply_fusion.2
  1002.7 18.0 %psum.7 = f32[512]{0:T(512)S(1)} all-reduce(f32[512]{0:T(512)S(1)} %get-tuple-element.8), channel_id=1, replica_groups=mesh['src'=32,'freq'=8] {'freq'}, use_global_device_ids=true, to_apply=%region_5.6 | all-reduce | flops 512 | bytes 4096 | tf_op jit(solution)/shard_map/psum | solution.py:122
  1020.7 1.3 fusion.59
  (38 shorter events, 1.6 us)
Async XLA Ops:
  7.2 751.7 %all-reduce.3.cloned.1.call-start = ((), (), s32[]{:S(2)}) async-start(), calls=%async_computation.3 | async-start | bytes 8388608
  8.9 31.7 %copy-start.8 = (s32[32]{0:T(128)S(1)}, s32[32]{0:T(128)}, u32[]{:S(2)}) copy-start(s32[32]{0:T(128)} %param.11) | copy-start | bytes 388
  8.9 32.3 %copy-start.4 = (f32[512]{0:T(512)S(1)}, f32[512]{0:T(512)}, u32[]{:S(2)}) copy-start(f32[512]{0:T(512)} %param.9) | copy-start | bytes 6148
  8.9 33.0 %copy-start.2 = (f32[32,512]{1,0:T(8,128)S(1)}, f32[32,512]{1,0:T(8,128)}, u32[]{:S(2)}) copy-start(f32[32,512]{1,0:T(8,128)} %param.10) | copy-start | bytes 196612
  68.4 19.8 %copy-start.3 = (s32[2,4096]{1,0:T(2,128)S(1)}, s32[2,4096]{1,0:T(2,128)}, u32[]{:S(2)}) copy-start(s32[2,4096]{1,0:T(2,128)} %param.13) | copy-start | bytes 98308
  307.3 2.2 copy-start
  307.3 2.9 copy-start.1
  327.3 0.7 copy-start.9
  327.3 467.9 %copy-start.6 = (f32[2,256,16]{1,2,0:T(8,128)S(1)}, f32[2,256,16]{1,2,0:T(8,128)}, u32[]{:S(2)}) copy-start(f32[2,256,16]{1,2,0:T(8,128)} %param.14) | copy-start | bytes 98308
  327.3 467.9 %copy-start.7 = (f32[256]{0:T(256)S(1)}, f32[256]{0:T(256)}, u32[]{:S(2)}) copy-start(f32[256]{0:T(256)} %param.15) | copy-start | bytes 3076
  760.5 30.4 %all-to-all-start = ((f32[8,1,1024]{2,1,0:T(1,128)}), f32[8,1,1024]{2,1,0:T(1,128)S(1)}, u32[]{:S(2)}, u32[]{:S(2)}) async-start(f32[8,1,1024]{2,1,0:T(1,128)} %reshape.337), calls=%async_computation | async-start | bytes 65536 | tf_op jit(solution)/shard_map/all_to_all | solution.py:115
  785.9 133.1 %all-gather.2.cloned.1.call-start = ((), (), s32[]{:S(2)}) async-start(), calls=%async_computation.2 | async-start | bytes 4325376 | tf_op jit(solution)/shard_map/all_gather | solution.py:118
  800.2 13.3 %copy-start.5 = (s32[2]{0:T(128)S(1)}, s32[2]{0:T(128)}, u32[]{:S(2)}) copy-start(s32[2]{0:T(128)} %constant.70) | copy-start | bytes 28
Sparse Core Ops, SparseCore 0:
  327.4 431.3 all-reduce.2
  813.6 105.4 all-gather.1
where the time goes:
time: 1040 us; the launch traced here: 1030 us
  waiting for transfers between devices  540 us (52%)
  local copies, waits for them, and re-layouts  275 us (26%)
  other arithmetic  89.9 us (9%)
  matrix products  57 us (5%)
  blocking collectives  26.3 us (3%)
  starting transfers between devices  25.4 us (2%)
  between operations  15.2 us (1%)
    unnamed x3, waiting for transfers between devices  430 us
    all_gather x1, waiting for transfers between devices, body(): full_cot = lax.all_gather(returned, 'src', axis=2, tiled=True)  105 us
    gather x1, local copies, waits for them, and re-layouts, baseline_values(): inner_product_matrix[:, antenna_left, antenna_right]  59.6 us
    gather x1, local copies, waits for them, and re-layouts, baseline_values(): inner_product_matrix[:, antenna_left + antenna_total, antenna_right]  59.5 us
    gather x1, local copies, waits for them, and re-layouts, baseline_values(): inner_product_matrix[:, antenna_left + antenna_total, antenna_right + ant...  59.4 us
    unnamed x5, other arithmetic  49.2 us
    gather x1, local copies, waits for them, and re-layouts, baseline_values(): inner_product_matrix[:, antenna_left, antenna_right + antenna_total]  40.4 us
    cos x1, other arithmetic, phase_matrix(): return jnp.concatenate([jnp.cos(phase), jnp.sin(phase)], axis=1)  31.6 us
  transfers between devices with their start and end apart: 3, of which 3 were waited for; matrix products, arithmetic and copies ran while one was open for 0% of the time, Pallas kernels for 0%

commit v1 on v0

v1 whole, which is shorter than its diff:
```python
import functools
import math

import jax
import jax.numpy as jnp
import numpy as np
from jax import lax
from jax.experimental import pallas as pl
from jax.experimental.pallas import tpu as pltpu
from jax.sharding import PartitionSpec as P

TWO_PI = 2.0 * math.pi
MESH = pl.DeviceIdType.MESH
F32 = jnp.float32
BF16 = jnp.bfloat16
LANES = 128
NT = (((1,), (1,)), ((), ()))
NN = (((1,), (0,)), ((), ()))
SIN_POLY = (6.283184916495431, -41.34158923268848, 81.59994332978007, -76.61447253122434, 41.34288235446963, -12.471243534886277)
COS_POLY = (0.9999999890590217, -19.73920449945381, 64.93911745989173, -85.45013953082399, 60.16763095051855, -25.967599246994247, 6.528658159389057)


def dot(left, right, dims=NN):
    return lax.dot_general(left, right, dims, preferred_element_type=F32)


def split(value):
    high = value.astype(BF16)
    return high, (value - high.astype(F32)).astype(BF16)


def horner(coefficients, variable):
    total = coefficients[-1] * variable + coefficients[-2]
    for coefficient in coefficients[-3::-1]:
        total = total * variable + coefficient
    return total


def sin_cos_turns(turns):
    rest = turns - jnp.round(turns)
    square = rest * rest
    return rest * horner(SIN_POLY, square), horner(COS_POLY, square)


def delay_tables(nch):
    index = np.arange(nch)
    angle = 2.0 * np.pi * ((index[:, None] * index[None, :]) % nch) / nch
    taper = 0.6 - 0.4 * np.cos(2.0 * np.pi * (index + 0.5) / nch)
    cos, sin = np.cos(angle) / math.sqrt(nch), np.sin(angle) / math.sqrt(nch)
    forward = np.zeros((2, nch, nch, 2))
    forward[0, :, :, 0] = cos
    forward[0, :, :, 1] = sin
    forward[1, :, :, 0] = -sin
    forward[1, :, :, 1] = cos
    forward *= taper[None, None, :, None]
    forward = forward.reshape(2 * nch, 2 * nch)
    return np.stack([forward, forward.T]).astype(np.float32)


def peer_at(own, step, count):
    if count != 32:
        return lax.rem(own + step, count)
    own_x, own_z, own_y = lax.rem(own, 4), lax.rem(own // 4, 2), own // 8
    x = lax.rem(own_x + lax.rem(step, 4), 4)
    y = lax.rem(own_y + lax.rem(step // 4, 4), 4)
    z = lax.rem(own_z + step // 16, 2)
    return y * 8 + z * 4 + x


def kernel(
    ns, nf, centre,
    dirs_ref, flux_ref, beam_ref, counts_ref, ant_ref, pairs_ref, data_ref, dw_ref, tables_hbm,
    u_ref, total_ref,
    source_send, source_recv, phased_hi, phased_lo, one_left, one_right, ant_cols, gram_ref,
    vis_send, vis_recv, vis_rows, vis_all, dat_recv, tables, cot_all, cot_rows, cot_send, cot_recv,
    u_send, u_recv, flux_send, flux_recv,
    table_sem, send1, recv1, send2, recv2, send3, recv3, send4, recv4, send5, recv5, send6, recv6, send7, recv7,
    send8, recv8,
):
    nch = ns * nf
    slots = dirs_ref.shape[1]
    nb = ns * LANES
    rows = 2 * ns
    s = lax.axis_index("src")
    q = lax.axis_index("freq")

    barrier = pltpu.get_barrier_semaphore()

    def greet_src(step, carry):
        pl.semaphore_signal(barrier, inc=1, device_id={"src": peer_at(s, step, ns)}, device_id_type=MESH)
        return carry

    def greet_freq(step, carry):
        pl.semaphore_signal(barrier, inc=1, device_id={"freq": lax.rem(q + step, nf)}, device_id_type=MESH)
        return carry

    lax.fori_loop(1, ns, greet_src, 0)
    lax.fori_loop(1, nf, greet_freq, 0)
    table_copy = pltpu.make_async_copy(tables_hbm, tables, table_sem)
    table_copy.start()

    along_l, along_m = dirs_ref[0:1, :], dirs_ref[1:2, :]
    along_n = jnp.sqrt(1.0 - along_l * along_l - along_m * along_m)
    live = lax.broadcasted_iota(jnp.int32, (1, slots), 1) < counts_ref[s]
    strength = jnp.where(live, jnp.sqrt(flux_ref[...] * (1.0 / math.sqrt(slots * ns))), 0.0)
    roots = beam_ref[...] * strength
    for i in range(ns):
        source_send[i, 0:1, :] = along_l
        source_send[i, 1:2, :] = along_m
        source_send[i, 2:3, :] = along_n
        source_send[i, 3:4, :] = roots[i : i + 1, :]
    source_recv[s] = source_send[s]

    pl.semaphore_wait(barrier, ns - 1 + nf - 1)

    def send_sources(step, carry):
        peer = peer_at(s, ns - step, ns)
        pltpu.make_async_remote_copy(
            src_ref=source_send.at[peer], dst_ref=source_recv.at[s], send_sem=send1, recv_sem=recv1.at[s],
            device_id={"src": peer}, device_id_type=MESH,
        ).start()
        return carry

    lax.fori_loop(1, ns, send_sources, 0)

    @pl.when(q == centre)
    def _():
        dat_recv[q] = data_ref[...]

    @pl.when(q != centre)
    def _():
        pltpu.make_async_remote_copy(
            src_ref=data_ref, dst_ref=dat_recv.at[q], send_sem=send2, recv_sem=recv2.at[q],
            device_id={"freq": centre}, device_id_type=MESH,
        ).start()

    freq = 1.0 + 0.6 * (q * ns + s).astype(F32) / nch
    for i in range(3):
        ant_cols[i] = jnp.transpose(jnp.broadcast_to(ant_ref[i : i + 1, :] * freq, (LANES, LANES)))

    antenna_id = lax.broadcasted_iota(jnp.int32, (LANES, 512), 0)

    def build_one_hot(j, carry):
        at = pl.ds(pl.multiple_of(j * 512, 512), 512)
        one_left[:, at] = (antenna_id == pairs_ref[0:1, at]).astype(F32).astype(BF16)
        one_right[:, at] = (antenna_id == pairs_ref[1:2, at]).astype(F32).astype(BF16)
        return carry

    lax.fori_loop(0, nb // 512, build_one_hot, 0)

    gram_ref[...] = jnp.zeros_like(gram_ref)

    def forward(step, carry):
        k = peer_at(s, step, ns)

        @pl.when(step > 0)
        def _():
            pltpu.make_async_remote_copy(
                src_ref=source_send.at[k], dst_ref=source_recv.at[k], send_sem=send1, recv_sem=recv1.at[k],
                device_id={"src": k}, device_id_type=MESH,
            ).wait_recv()

        for lane in range(0, slots, LANES):
            at = pl.ds(lane, LANES)
            row_l, row_m = source_recv[k, 0:1, at], source_recv[k, 1:2, at]
            row_n, root = source_recv[k, 2:3, at], source_recv[k, 3:4, at]
            for first in range(0, LANES, 64):
                ants = pl.ds(first, 64)
                turns = ant_cols[0, ants, :] * row_l + ant_cols[1, ants, :] * row_m + ant_cols[2, ants, :] * row_n
                sine, cosine = sin_cos_turns(turns)
                for base, value in ((0, cosine * root), (LANES, sine * root)):
                    high = value.astype(BF16)
                    phased_hi[k, pl.ds(base + first, 64), at] = high
                    phased_lo[k, pl.ds(base + first, 64), at] = (2.0 * (value - high.astype(F32))).astype(BF16)
        high = phased_hi[k]
        gram_ref[...] += dot(high, high, NT) + dot(high, phased_lo[k], NT)
        return carry

    lax.fori_loop(0, ns, forward, 0)

    gram = gram_ref[...]
    even = gram[:LANES, :LANES] + gram[LANES:, LANES:]
    odd = gram[LANES:, :LANES] - gram[:LANES, LANES:]
    vis_re = 0.5 * (even + even.T)
    vis_im = 0.5 * (odd - odd.T)
    grid_hi, grid_lo = split(jnp.concatenate([vis_re, -vis_im], axis=0))

    def gather(j, carry):
        at = pl.ds(pl.multiple_of(j * 512, 512), 512)
        left = one_left[:, at]
        picked = dot(grid_hi, left) + dot(grid_lo, left)
        right = one_right[:, at].astype(F32)
        real = jnp.sum(picked[:LANES] * right, axis=0, keepdims=True)
        imag = jnp.sum(picked[LANES:] * right, axis=0, keepdims=True)
        for i in range(4):
            vis_send[j * 4 + i, 0:1, :] = real[:, i * LANES : (i + 1) * LANES]
            vis_send[j * 4 + i, 1:2, :] = imag[:, i * LANES : (i + 1) * LANES]
        return carry

    lax.fori_loop(0, nb // 512, gather, 0)

    def send_vis(step, carry):
        peer = peer_at(s, ns - step, ns)
        pltpu.make_async_remote_copy(
            src_ref=vis_send.at[peer], dst_ref=vis_recv.at[s], send_sem=send3, recv_sem=recv3,
            device_id={"src": peer}, device_id_type=MESH,
        ).start()
        return carry

    lax.fori_loop(1, ns, send_vis, 0)
    vis_recv[s] = vis_send[s]
    most = pl.ds(0, ns - 1)
    pltpu.make_async_copy(vis_send.at[most], vis_recv.at[most], recv3).wait()
    for i in range(ns):
        vis_rows[2 * i : 2 * i + 2, :] = vis_recv[i]

    @pl.when(q != centre)
    def _():
        pltpu.make_async_remote_copy(
            src_ref=vis_rows, dst_ref=vis_all.at[q], send_sem=send4, recv_sem=recv4.at[q],
            device_id={"freq": centre}, device_id_type=MESH,
        ).start()

    table_copy.wait()

    @pl.when(q == centre)
    def _():
        vis_all[q] = vis_rows[...]

        def take_data(step, carry):
            other = lax.rem(q + step, nf)
            pltpu.make_async_remote_copy(
                src_ref=data_ref, dst_ref=dat_recv.at[other], send_sem=send2, recv_sem=recv2.at[other],
                device_id={"freq": other}, device_id_type=MESH,
            ).wait_recv()
            return carry

        lax.fori_loop(1, nf, take_data, 0)
        weight = jnp.transpose(jnp.broadcast_to(dw_ref[...], (LANES, nch)))
        spectra = [
            jnp.transpose(jnp.concatenate([dat_recv[i, c] for i in range(nf)], axis=0)) for c in range(2)
        ]

        there_hi, there_lo = split(tables[0])
        back_hi, back_lo = split(tables[1])

        def take_vis(step, carry):
            other = lax.rem(q + step, nf)
            pltpu.make_async_remote_copy(
                src_ref=vis_rows, dst_ref=vis_all.at[other], send_sem=send4, recv_sem=recv4.at[other],
                device_id={"freq": other}, device_id_type=MESH,
            ).wait_recv()
            return carry

        lax.fori_loop(1, nf, take_vis, 0)
        vis_hi, vis_lo = split(jnp.concatenate([vis_all[i] for i in range(nf)], axis=0))
        spec = dot(there_hi, vis_hi) + dot(there_hi, vis_lo) + dot(there_lo, vis_hi)
        spec_cot = jnp.concatenate(
            [weight * (spec[:nch] - spectra[0]), weight * (spec[nch:] - spectra[1])], axis=0
        )
        cot_hi, cot_lo = split(spec_cot)
        back = dot(back_hi, cot_hi) + dot(back_hi, cot_lo) + dot(back_lo, cot_hi)
        for i in range(nf):
            cot_all[i] = back[i * rows : (i + 1) * rows]

        def send_cot(step, carry):
            other = lax.rem(q + step, nf)
            pltpu.make_async_remote_copy(
                src_ref=cot_all.at[other], dst_ref=cot_rows, send_sem=send5, recv_sem=recv5,
                device_id={"freq": other}, device_id_type=MESH,
            ).start()
            return carry

        lax.fori_loop(1, nf, send_cot, 0)
        cot_rows[...] = cot_all[q]

    @pl.when(q != centre)
    def _():
        pltpu.make_async_remote_copy(
            src_ref=cot_all.at[q], dst_ref=cot_rows, send_sem=send5, recv_sem=recv5,
            device_id={"freq": centre}, device_id_type=MESH,
        ).wait_recv()

    for i in range(ns):
        cot_send[i] = cot_rows[2 * i : 2 * i + 2, :]

    def fan_out(step, carry):
        peer = peer_at(s, ns - step, ns)
        pltpu.make_async_remote_copy(
            src_ref=cot_send.at[peer], dst_ref=cot_recv.at[s], send_sem=send6, recv_sem=recv6,
            device_id={"src": peer}, device_id_type=MESH,
        ).start()
        return carry

    lax.fori_loop(1, ns, fan_out, 0)
    cot_recv[s] = cot_send[s]
    pltpu.make_async_copy(cot_send.at[most], cot_recv.at[most], recv6).wait()

    def scatter(j, total):
        at = pl.ds(pl.multiple_of(j * 512, 512), 512)
        right = one_right[:, at]
        parts = []
        for c in range(2):
            row = jnp.concatenate([cot_recv[j * 4 + i, c : c + 1, :] for i in range(4)], axis=1)
            parts.append(split(row))
        scaled = [right * parts[c][part] for part in range(2) for c in range(2)]
        return total + dot(one_left[:, at], jnp.concatenate(scaled, axis=0), NT)

    grids = lax.fori_loop(0, nb // 512, scatter, jnp.zeros((LANES, 4 * LANES), F32))
    grids = grids[:, : 2 * LANES] + grids[:, 2 * LANES :]
    real, imag = grids[:, :LANES], grids[:, LANES:]
    real, imag = 0.5 * (real + real.T), 0.5 * (imag - imag.T)
    matrix = jnp.concatenate(
        [jnp.concatenate([real, -imag], axis=1), jnp.concatenate([imag, real], axis=1)], axis=0
    )
    matrix_hi, matrix_lo = split(matrix)
    gram_ref[...] = matrix

    def backward(step, carry):
        k = peer_at(s, ns - step, ns)
        high = phased_hi[k]
        product = dot(matrix_hi, high) + dot(matrix_lo, high)
        phased = high.astype(F32) + phased_lo[k].astype(F32)
        u_send[k] = jnp.sum(phased * product, axis=0, keepdims=True)

        @pl.when(step < ns)
        def _():
            pltpu.make_async_remote_copy(
                src_ref=u_send.at[k], dst_ref=u_recv.at[s], send_sem=send7, recv_sem=recv7,
                device_id={"src": k}, device_id_type=MESH,
            ).start()

        return carry

    lax.fori_loop(1, ns + 1, backward, 0)
    u_recv[s] = u_send[s]
    pltpu.make_async_copy(u_send.at[most], u_recv.at[most], recv7).wait()
    for i in range(ns):
        u_ref[i : i + 1, :] = u_recv[i]
    flux_send[0] = jnp.sum(u_ref[...], axis=0, keepdims=True)

    def send_flux(step, carry):
        other = lax.rem(q + step, nf)
        pltpu.make_async_remote_copy(
            src_ref=flux_send, dst_ref=flux_recv.at[pl.ds(q, 1)], send_sem=send8, recv_sem=recv8,
            device_id={"freq": other}, device_id_type=MESH,
        ).start()
        return carry

    lax.fori_loop(1, nf, send_flux, 0)
    flux_recv[q] = flux_send[0]
    others = pl.ds(0, nf - 1)
    pltpu.make_async_copy(flux_recv.at[others], flux_recv.at[others], recv8).wait()
    total = flux_recv[0]
    for i in range(1, nf):
        total = total + flux_recv[i]
    total_ref[...] = total

    pltpu.make_async_copy(source_send.at[most], source_recv.at[most], send1).wait()
    pltpu.make_async_copy(vis_send.at[most], vis_recv.at[most], send3).wait()
    pltpu.make_async_copy(cot_send.at[most], cot_recv.at[most], send6).wait()
    pltpu.make_async_copy(u_send.at[most], u_recv.at[most], send7).wait()
    pltpu.make_async_copy(flux_recv.at[others], flux_recv.at[others], send8).wait()

    @pl.when(q == centre)
    def _():
        pltpu.make_async_copy(cot_all.at[others], cot_all.at[others], send5).wait()

    @pl.when(q != centre)
    def _():
        pltpu.make_async_copy(data_ref, dat_recv.at[0], send2).wait()
        pltpu.make_async_copy(vis_rows, vis_rows, send4).wait()


def body(source_dirs, flux, beam, counts, antennas, pairs, data, delay_weight):
    ns, nf = lax.axis_size("src"), lax.axis_size("freq")
    slots = flux.shape[0]
    nch = ns * nf
    share = LANES // nf
    rows = 2 * ns
    vmem, smem = pl.BlockSpec(memory_space=pltpu.VMEM), pl.BlockSpec(memory_space=pltpu.SMEM)
    dma = pltpu.SemaphoreType.DMA
    macs = 4 * ns * slots * 256 * 256
    gradient, total = pl.pallas_call(
        functools.partial(kernel, ns, nf, min(3, nf - 1)),
        out_shape=(
            jax.ShapeDtypeStruct((ns, slots), F32),
            jax.ShapeDtypeStruct((1, slots), F32),
        ),
        in_specs=[vmem, vmem, vmem, smem, vmem, vmem, vmem, vmem, pl.BlockSpec(memory_space=pltpu.HBM)],
        out_specs=(vmem, vmem),
        scratch_shapes=[
            pltpu.VMEM((ns, 4, slots), F32),
            pltpu.VMEM((ns, 4, slots), F32),
            pltpu.VMEM((ns, 2 * LANES, slots), BF16),
            pltpu.VMEM((ns, 2 * LANES, slots), BF16),
            pltpu.VMEM((LANES, ns * LANES), BF16),
            pltpu.VMEM((LANES, ns * LANES), BF16),
            pltpu.VMEM((3, LANES, LANES), F32),
            pltpu.VMEM((2 * LANES, 2 * LANES), F32),
            pltpu.VMEM((ns, 2, LANES), F32),
            pltpu.VMEM((ns, 2, LANES), F32),
            pltpu.VMEM((rows, LANES), F32),
            pltpu.VMEM((nf, rows, LANES), F32),
            pltpu.VMEM((nf, 2, share, nch), F32),
            pltpu.VMEM((2, 2 * nch, 2 * nch), F32),
            pltpu.VMEM((nf, rows, LANES), F32),
            pltpu.VMEM((rows, LANES), F32),
            pltpu.VMEM((ns, 2, LANES), F32),
            pltpu.VMEM((ns, 2, LANES), F32),
            pltpu.VMEM((ns, 1, slots), F32),
            pltpu.VMEM((ns, 1, slots), F32),
            pltpu.VMEM((1, 1, slots), F32),
            pltpu.VMEM((nf, 1, slots), F32),
            dma,
            dma, dma((ns,)),
            dma, dma((nf,)),
            dma, dma,
            dma, dma((nf,)),
            dma, dma,
            dma, dma,
            dma, dma,
            dma, dma,
        ],
        compiler_params=pltpu.CompilerParams(
            collective_id=0, has_side_effects=True, vmem_limit_bytes=48 * 1024 * 1024
        ),
        cost_estimate=pl.CostEstimate(flops=2 * macs, bytes_accessed=4 * 1024 * 1024, transcendentals=0),
    )(
        source_dirs, flux[None, :], beam, counts, antennas, pairs, jnp.transpose(data, (0, 2, 1)), delay_weight[None, :],
        jnp.asarray(delay_tables(nch)),
    )
    return (total[0] / flux, 2.0 * gradient / beam)


def solution(mesh):
    in_specs = (
        P(None, "src"),
        P("src"),
        P("freq", "src"),
        P(),
        P(),
        P(),
        P(None, None, ("src", "freq")),
        P(),
    )
    out_specs = (P("src"), P("freq", "src"))
    return jax.shard_map(body, mesh=mesh, in_specs=in_specs, out_specs=out_specs, check_vma=False)
```

time: 1040 us -> 96.7 us (0.09); the launches traced: 1030 us -> 96.3 us
  waiting for transfers between devices: 540 us -> 0 us
  local copies, waits for them, and re-layouts: 275 us -> 7.32 us
  other arithmetic: 89.9 us -> 1.23 us
  Pallas kernels: 0 us -> 87.1 us
  matrix products: 57 us -> 0 us
  blocking collectives: 26.3 us -> 0 us
  starting transfers between devices: 25.4 us -> 0 us
  between operations: 15.2 us -> 0.66 us
    unnamed x3 -> x0, waiting for transfers between devices: 430 us -> none
    gather x4 -> x0, local copies, waits for them, and re-layouts: 219 us -> none  [the longest x1 59.6 us: baseline_values(): inner_product_matrix[:, antenna_left, antenna_right]]
    all_gather x1 -> x0, waiting for transfers between devices: 105 us -> none  [body(): full_cot = lax.all_gather(returned, 'src', axis=2, tiled=True)]
    pallas_call x0 -> x1, Pallas kernels: none -> 87.1 us  [body(): pl.pallas_call(functools.partial(kernel, ns, nf, min(3, nf - 1)), out_sha...]
    dot_general x10 -> x0, matrix products: 57 us -> none  [the longest x1 26.4 us: gram_of(): jnp.einsum('cas,cbs->cab', phased * weights[:, None, :], phased, precisio...]
    unnamed x5 -> x0, other arithmetic: 49.2 us -> none
    cos x1 -> x0, other arithmetic: 31.6 us -> none  [phase_matrix(): return jnp.concatenate([jnp.cos(phase), jnp.sin(phase)], axis=1)]
    all_to_all x1 -> x0, starting transfers between devices: 25.4 us -> none  [body(): lax.all_to_all(shares, 'freq', split_axis=2, concat_axis=1, tiled=True)]
  transfers between devices with their start and end apart: 3 -> 0, of which waited for: 3 -> 0; matrix products, arithmetic and copies ran while one was open for 0% -> 0% of each run, Pallas kernels for 0% -> 0%
where the time goes in v1:
time: 96.7 us; the launch traced here: 96.3 us
  Pallas kernels  87.1 us (90%)
  local copies, waits for them, and re-layouts  7.32 us (8%)
  other arithmetic  1.23 us (1%)
    pallas_call x1, Pallas kernels, body(): pl.pallas_call(functools.partial(kernel, ns, nf, min(3, nf - 1)), out_sha...  87.1 us
    unnamed x18, local copies, waits for them, and re-layouts  7.32 us

profile of v1, /device:TPU:1, one launch (start us, length us, event | category | flops | bytes accessed | tf_op | source)
XLA Modules:
  0.0 96.3 jit_solution(14522240366331283499)
XLA Ops:
  0.6 0.0 copy-start
  0.6 0.8 copy-done
  1.5 0.0 copy-start.1
  1.5 0.7 copy-done.1
  2.2 0.0 copy-start.2
  2.2 0.8 copy-done.2
  2.9 0.0 copy-start.3
  2.9 0.8 copy-done.3
  3.7 0.0 copy-start.4
  3.7 0.7 copy-done.4
  4.4 0.0 copy-start.5
  4.4 0.7 copy-done.5
  5.0 0.0 copy-start.6
  5.0 0.7 copy-done.6
  5.7 0.0 copy-start.7
  5.7 0.7 copy-done.7
  6.4 0.0 copy-start.8
  6.4 1.6 %copy-done.8 = f32[2,512,512]{2,1,0:T(8,128)S(1)} copy-done((f32[2,512,512]{2,1,0:T(8,128)S(1)}, f32[2,512,512]{2,1,0:T(8,128)}, u32[]{:S(2)}) %copy-start.8) | copy-done | bytes 2097176
  8.0 87.1 %shard_map.104 = (f32[32,512]{1,0:T(8,128)S(1)}, f32[1,512]{1,0:T(1,128)S(1)}) custom-call(f32[2,512]{1,0:T(2,128)S(1)} %copy-done.4, f32[1,512]{1,0:T(1,128)S(1)} %bitcast.4, f32[32,512]{1,0:T(8,128)S(1)} %copy-done, s32[32]{0:T(128)S(1)} %copy-done.7, f32[3,128]{1,0:T(4,128)S(1)} %copy-done.5, s32[2,4096]{1,0:T(2,128)S(1)} %copy-done.2, ...), custom_call_target="tpu_custom_call" | custom-call | flops 8589934592 | bytes 4194304 | tf_op jit(solution)/shard_map/pallas_call | solution.py:384
  95.1 0.6 div.6
  95.6 0.6 multiply_divide_fusion
Async XLA Ops:
  0.6 0.8 copy-start
  1.5 0.7 copy-start.1
  2.2 0.8 copy-start.2
  2.9 0.8 copy-start.3
  3.7 0.7 copy-start.4
  4.4 0.7 copy-start.5
  5.0 0.7 copy-start.6
  5.7 0.7 copy-start.7
  6.4 1.6 %copy-start.8 = (f32[2,512,512]{2,1,0:T(8,128)S(1)}, f32[2,512,512]{2,1,0:T(8,128)}, u32[]{:S(2)}) copy-start(f32[2,512,512]{2,1,0:T(8,128)} %constant.4.clone.tables_hbm) | copy-start | bytes 6291460

commit v2 on v1

v2 whole, which is shorter than its diff:
```python
import functools
import math

import jax
import jax.numpy as jnp
import numpy as np
from jax import lax
from jax.experimental import pallas as pl
from jax.experimental.pallas import tpu as pltpu
from jax.sharding import PartitionSpec as P

TWO_PI = 2.0 * math.pi
MESH = pl.DeviceIdType.MESH
F32 = jnp.float32
BF16 = jnp.bfloat16
LANES = 128
NT = (((1,), (1,)), ((), ()))
NN = (((1,), (0,)), ((), ()))
SIN_POLY = (3.141592640130707, -5.167710083507862, 2.550077523214134, -0.5982912856178576, 0.0776576603009221)
COS_POLY = (0.9999999532476082, -4.93479283061961, 4.058411352862035, -1.3318765680776314, 0.2196896110917421)


def dot(left, right, dims=NN):
    return lax.dot_general(left, right, dims, preferred_element_type=F32)


def split(value):
    high = value.astype(BF16)
    return high, (value - high.astype(F32)).astype(BF16)


def horner(coefficients, variable):
    total = coefficients[-1] * variable + coefficients[-2]
    for coefficient in coefficients[-3::-1]:
        total = total * variable + coefficient
    return total


def scaled_cos_sin(turns, root):
    rest = turns - jnp.round(turns)
    square = rest * rest
    sine = rest * horner(SIN_POLY, square)
    twice = (2.0 * root) * sine
    return root - twice * sine, twice * horner(COS_POLY, square)


def three_parts(value):
    first = value.astype(BF16).astype(F32)
    rest = value - first
    second = rest.astype(BF16).astype(F32)
    return first, second, (rest - second).astype(BF16).astype(F32)


def delay_tables(nch):
    index = np.arange(nch)
    angle = 2.0 * np.pi * ((index[:, None] * index[None, :]) % nch) / nch
    taper = 0.6 - 0.4 * np.cos(2.0 * np.pi * (index + 0.5) / nch)
    cos, sin = np.cos(angle) / math.sqrt(nch), np.sin(angle) / math.sqrt(nch)
    forward = np.zeros((2, nch, nch, 2))
    forward[0, :, :, 0] = cos
    forward[0, :, :, 1] = sin
    forward[1, :, :, 0] = -sin
    forward[1, :, :, 1] = cos
    forward *= taper[None, None, :, None]
    forward = forward.reshape(2 * nch, 2 * nch)
    return np.stack([forward, forward.T]).astype(np.float32)


def peer_at(own, step, count):
    if count != 32:
        return lax.rem(own + step, count)
    own_x, own_z, own_y = lax.rem(own, 4), lax.rem(own // 4, 2), own // 8
    x = lax.rem(own_x + lax.rem(step, 4), 4)
    y = lax.rem(own_y + lax.rem(step // 4, 4), 4)
    z = lax.rem(own_z + step // 16, 2)
    return y * 8 + z * 4 + x


def quad_at(own, step, count):
    if count != 8:
        return lax.rem(own + step, count)
    y = lax.rem(own // 2 + lax.rem(step, 4), 4)
    z = lax.rem(lax.rem(own, 2) + step // 4, 2)
    return y * 2 + z


def kernel(
    ns, nf, centre,
    dirs_hbm, flux_hbm, beam_hbm, counts_hbm, ant_hbm, pairs_hbm, data_hbm, dw_hbm, tables_hbm,
    u_ref, total_ref,
    dirs_ref, flux_ref, beam_ref, counts_ref, ant_ref, pairs_ref, data_ref, dw_ref, tables,
    source_send, source_recv, phased_hi, phased_lo, left_twice, one_right, ant_parts, even_hi, even_lo, odd_hi, odd_lo, gram_hh, gram_hl,
    vis_send, vis_recv, vis_rows, vis_all, dat_recv, tables_hi, tables_lo, cot_all, cot_rows, cot_send, cot_recv,
    u_send, u_recv, flux_send, flux_recv,
    input_sem, send1, recv1, send2, recv2, send3, recv3, send4, recv4, send5, recv5, send6, recv6, send7, recv7,
    send8, recv8,
):
    nch = ns * nf
    slots = dirs_ref.shape[1]
    nb = ns * LANES
    rows = 2 * ns
    s = lax.axis_index("src")
    q = lax.axis_index("freq")

    inputs = [
        pltpu.make_async_copy(hbm, vmem, input_sem.at[i])
        for i, (hbm, vmem) in enumerate((
            (dirs_hbm, dirs_ref), (flux_hbm, flux_ref), (beam_hbm, beam_ref), (counts_hbm, counts_ref),
            (ant_hbm, ant_ref), (pairs_hbm, pairs_ref), (data_hbm, data_ref), (dw_hbm, dw_ref),
            (tables_hbm, tables),
        ))
    ]
    for copy in inputs:
        copy.start()
    barrier = pltpu.get_barrier_semaphore()

    def greet_src(step, carry):
        pl.semaphore_signal(barrier, inc=1, device_id={"src": peer_at(s, ns - step, ns)}, device_id_type=MESH)
        return carry

    def greet_freq(step, carry):
        pl.semaphore_signal(barrier, inc=1, device_id={"freq": lax.rem(q + step, nf)}, device_id_type=MESH)
        return carry

    lax.fori_loop(1, ns, greet_src, 0)
    lax.fori_loop(1, nf, greet_freq, 0)
    for copy in inputs[:8]:
        copy.wait()

    along_l, along_m = dirs_ref[0:1, :], dirs_ref[1:2, :]
    along_n = jnp.sqrt(1.0 - along_l * along_l - along_m * along_m)
    live = lax.broadcasted_iota(jnp.int32, (1, slots), 1) < counts_ref[s]
    strength = jnp.where(live, jnp.sqrt(flux_ref[...] * (1.0 / math.sqrt(slots * ns))), 0.0)
    roots = beam_ref[...] * strength
    for i in range(ns):
        source_send[i, 0:1, :] = along_l
        source_send[i, 1:2, :] = along_m
        source_send[i, 2:3, :] = along_n
        source_send[i, 3:4, :] = roots[i : i + 1, :]
    source_recv[s] = source_send[s]

    freq = 1.0 + 0.6 * (q * ns + s).astype(F32) / nch
    first, second, third = three_parts(
        jnp.concatenate([ant_ref[...] * freq, jnp.zeros((5, LANES), F32)], axis=0)
    )
    spare = jnp.zeros((LANES - 48, LANES), F32)
    ant_parts[...] = jnp.transpose(
        jnp.concatenate([first, second, third, first, second, first, spare], axis=0)
    ).astype(BF16)

    gram_hh[...] = jnp.zeros_like(gram_hh)
    gram_hl[...] = jnp.zeros_like(gram_hl)

    def expand(k, high_ref, low_ref):
        source = jnp.concatenate([source_recv[k], jnp.zeros((4, slots), F32)], axis=0)
        first, second, third = three_parts(source)
        parts = jnp.concatenate([first, first, first, second, second, third], axis=0).astype(BF16)
        turns = dot(ant_parts[:, :48], parts)
        for lane in range(0, slots, LANES):
            root = source_recv[k, 3:4, pl.ds(lane, LANES)]
            for top in range(0, LANES, 64):
                cosine, sine = scaled_cos_sin(turns[top : top + 64, lane : lane + LANES], root)
                for base, value in ((0, cosine), (LANES, sine)):
                    high, low = split(value)
                    at = (pl.ds(base + top, 64), pl.ds(lane, LANES))
                    phased_hi[(k, *at)] = high
                    phased_lo[(k, *at)] = low
                    high_ref[at] = high
                    low_ref[at] = low

    def correlate(high_ref, low_ref):
        high = high_ref[...]
        gram_hh[...] += dot(high, high, NT)
        gram_hl[...] += dot(high, low_ref[...], NT)

    expand(s, even_hi, even_lo)

    antenna_id = lax.broadcasted_iota(jnp.int32, (LANES, 512), 0)

    def build_one_hot(j, carry):
        at = pl.ds(pl.multiple_of(j * 512, 512), 512)
        left = (antenna_id == pairs_ref[0:1, at]).astype(F32).astype(BF16)
        left_twice[:LANES, at] = left
        left_twice[LANES:, at] = left
        one_right[:, at] = (antenna_id == pairs_ref[1:2, at]).astype(F32).astype(BF16)
        return carry

    lax.fori_loop(0, nb // 512, build_one_hot, 0)
    inputs[8].wait()

    @pl.when(q == centre)
    def _():
        piece = min(64, 2 * nch)

        def split_tables(j, carry):
            at = pl.ds(pl.multiple_of(j * piece, piece), piece)
            for i in range(2):
                tables_hi[i, at, :], tables_lo[i, at, :] = split(tables[i, at, :])
            return carry

        lax.fori_loop(0, 2 * nch // piece, split_tables, 0)

    pl.semaphore_wait(barrier, ns - 1 + nf - 1)

    def send_sources(step, carry):
        peer = peer_at(s, ns - step, ns)
        pltpu.make_async_remote_copy(
            src_ref=source_send.at[peer], dst_ref=source_recv.at[s], send_sem=send1, recv_sem=recv1.at[s],
            device_id={"src": peer}, device_id_type=MESH,
        ).start()
        return carry

    lax.fori_loop(1, ns, send_sources, 0)

    @pl.when(q == centre)
    def _():
        dat_recv[q] = data_ref[...]

    @pl.when(q != centre)
    def _():
        pltpu.make_async_remote_copy(
            src_ref=data_ref, dst_ref=dat_recv.at[q], send_sem=send2, recv_sem=recv2.at[q],
            device_id={"freq": centre}, device_id_type=MESH,
        ).start()

    def arrival(step):
        k = peer_at(s, step, ns)
        pltpu.make_async_remote_copy(
            src_ref=source_send.at[k], dst_ref=source_recv.at[k], send_sem=send1, recv_sem=recv1.at[k],
            device_id={"src": k}, device_id_type=MESH,
        ).wait_recv()
        return k

    def forward(pair, carry):
        k = arrival(2 * pair + 1)
        later = arrival(2 * pair + 2)
        expand(k, odd_hi, odd_lo)
        correlate(even_hi, even_lo)
        expand(later, even_hi, even_lo)
        correlate(odd_hi, odd_lo)
        return carry

    lax.fori_loop(0, ns // 2 - 1, forward, 0)
    expand(arrival(ns - 1), odd_hi, odd_lo)
    correlate(even_hi, even_lo)
    correlate(odd_hi, odd_lo)

    gram = gram_hh[...] + 2.0 * gram_hl[...]
    even = gram[:LANES, :LANES] + gram[LANES:, LANES:]
    odd = gram[LANES:, :LANES] - gram[:LANES, LANES:]
    vis_re = 0.5 * (even + even.T)
    vis_im = 0.5 * (odd - odd.T)
    grid_hi, grid_lo = split(jnp.concatenate([vis_re, -vis_im], axis=0))
    grid_parts = jnp.concatenate([grid_hi, grid_lo], axis=1)

    def gather(step, carry):
        j = quad_at(s // 4, ns // 4 - 1 - step, ns // 4)
        at = pl.ds(pl.multiple_of(j * 512, 512), 512)
        picked = dot(grid_parts, left_twice[:, at])
        right = one_right[:, at].astype(F32)
        real = jnp.sum(picked[:LANES] * right, axis=0, keepdims=True)
        imag = jnp.sum(picked[LANES:] * right, axis=0, keepdims=True)
        for i in range(4):
            peer = j * 4 + i
            vis_send[peer, 0:1, :] = real[:, i * LANES : (i + 1) * LANES]
            vis_send[peer, 1:2, :] = imag[:, i * LANES : (i + 1) * LANES]

            @pl.when(peer != s)
            def _():
                pltpu.make_async_remote_copy(
                    src_ref=vis_send.at[peer], dst_ref=vis_recv.at[s], send_sem=send3, recv_sem=recv3,
                    device_id={"src": peer}, device_id_type=MESH,
                ).start()

        return carry

    lax.fori_loop(0, ns // 4, gather, 0)
    vis_recv[s] = vis_send[s]

    @pl.when(q == centre)
    def _():
        def take_data(step, carry):
            other = lax.rem(q + step, nf)
            pltpu.make_async_remote_copy(
                src_ref=data_ref, dst_ref=dat_recv.at[other], send_sem=send2, recv_sem=recv2.at[other],
                device_id={"freq": other}, device_id_type=MESH,
            ).wait_recv()
            return carry

        lax.fori_loop(1, nf, take_data, 0)

    most = pl.ds(0, ns - 1)
    pltpu.make_async_copy(vis_send.at[most], vis_recv.at[most], recv3).wait()
    for i in range(ns):
        vis_rows[2 * i : 2 * i + 2, :] = vis_recv[i]

    @pl.when(q != centre)
    def _():
        pltpu.make_async_remote_copy(
            src_ref=vis_rows, dst_ref=vis_all.at[q], send_sem=send4, recv_sem=recv4.at[q],
            device_id={"freq": centre}, device_id_type=MESH,
        ).start()

    @pl.when(q == centre)
    def _():
        vis_all[q] = vis_rows[...]

        def three_passes(i, high, low):
            both = dot(tables_hi[i], jnp.concatenate([high, low], axis=1))
            return both[:, :LANES] + both[:, LANES:] + dot(tables_lo[i], high)

        weight = jnp.transpose(jnp.broadcast_to(dw_ref[...], (LANES, nch)))
        spectra = [
            jnp.transpose(jnp.concatenate([dat_recv[i, c] for i in range(nf)], axis=0)) for c in range(2)
        ]

        def take_vis(step, carry):
            other = lax.rem(q + step, nf)
            pltpu.make_async_remote_copy(
                src_ref=vis_rows, dst_ref=vis_all.at[other], send_sem=send4, recv_sem=recv4.at[other],
                device_id={"freq": other}, device_id_type=MESH,
            ).wait_recv()
            return carry

        lax.fori_loop(1, nf, take_vis, 0)
        vis_hi, vis_lo = split(jnp.concatenate([vis_all[i] for i in range(nf)], axis=0))
        spec = three_passes(0, vis_hi, vis_lo)
        spec_cot = jnp.concatenate(
            [weight * (spec[:nch] - spectra[0]), weight * (spec[nch:] - spectra[1])], axis=0
        )
        cot_hi, cot_lo = split(spec_cot)
        back = three_passes(1, cot_hi, cot_lo)
        for i in range(nf):
            cot_all[i] = back[i * rows : (i + 1) * rows]

        def send_cot(step, carry):
            other = lax.rem(q + step, nf)
            pltpu.make_async_remote_copy(
                src_ref=cot_all.at[other], dst_ref=cot_rows, send_sem=send5, recv_sem=recv5,
                device_id={"freq": other}, device_id_type=MESH,
            ).start()
            return carry

        lax.fori_loop(1, nf, send_cot, 0)
        cot_rows[...] = cot_all[q]

    @pl.when(q != centre)
    def _():
        pltpu.make_async_remote_copy(
            src_ref=cot_all.at[q], dst_ref=cot_rows, send_sem=send5, recv_sem=recv5,
            device_id={"freq": centre}, device_id_type=MESH,
        ).wait_recv()

    for i in range(ns):
        cot_send[i] = cot_rows[2 * i : 2 * i + 2, :]

    def fan_out(step, carry):
        peer = peer_at(s, ns - step, ns)
        pltpu.make_async_remote_copy(
            src_ref=cot_send.at[peer], dst_ref=cot_recv.at[s], send_sem=send6, recv_sem=recv6.at[s // 4],
            device_id={"src": peer}, device_id_type=MESH,
        ).start()
        return carry

    lax.fori_loop(1, ns, fan_out, 0)
    cot_recv[s] = cot_send[s]

    def scatter(step, total):
        j = quad_at(s // 4, step, ns // 4)

        @pl.when(step == 0)
        def _():
            pltpu.make_async_copy(cot_send.at[pl.ds(0, 3)], cot_recv.at[pl.ds(0, 3)], recv6.at[j]).wait()

        @pl.when(step != 0)
        def _():
            pltpu.make_async_copy(cot_send.at[pl.ds(0, 4)], cot_recv.at[pl.ds(0, 4)], recv6.at[j]).wait()

        at = pl.ds(pl.multiple_of(j * 512, 512), 512)
        right = one_right[:, at]
        parts = []
        for c in range(2):
            row = jnp.concatenate([cot_recv[j * 4 + i, c : c + 1, :] for i in range(4)], axis=1)
            parts.append(split(row))
        scaled = [right * parts[c][part] for part in range(2) for c in range(2)]
        return total + dot(left_twice[:LANES, at], jnp.concatenate(scaled, axis=0), NT)

    grids = lax.fori_loop(0, ns // 4, scatter, jnp.zeros((LANES, 4 * LANES), F32))
    grids = grids[:, : 2 * LANES] + grids[:, 2 * LANES :]
    real, imag = grids[:, :LANES], grids[:, LANES:]
    real, imag = 0.5 * (real + real.T), 0.5 * (imag - imag.T)
    matrix = jnp.concatenate(
        [jnp.concatenate([real, -imag], axis=1), jnp.concatenate([imag, real], axis=1)], axis=0
    )
    matrix_hi, matrix_lo = split(matrix)

    def pull_back(k):
        for lane in range(0, slots, 256):
            at = pl.ds(lane, 256)
            high = phased_hi[k, :, at]
            product = dot(matrix_hi, high) + dot(matrix_lo, high)
            phased = high.astype(F32) + 2.0 * phased_lo[k, :, at].astype(F32)
            u_send[k, :, at] = jnp.sum(phased * product, axis=0, keepdims=True)

    def send_gradient(k):
        pltpu.make_async_remote_copy(
            src_ref=u_send.at[k], dst_ref=u_recv.at[s], send_sem=send7, recv_sem=recv7,
            device_id={"src": k}, device_id_type=MESH,
        ).start()

    def backward(pair, carry):
        k = peer_at(s, ns - 1 - 2 * pair, ns)
        later = peer_at(s, ns - 2 - 2 * pair, ns)
        pull_back(k)
        pull_back(later)
        send_gradient(k)
        send_gradient(later)
        return carry

    lax.fori_loop(0, ns // 2 - 1, backward, 0)
    k = peer_at(s, 1, ns)
    pull_back(k)
    send_gradient(k)
    pull_back(s)
    u_recv[s] = u_send[s]
    pltpu.make_async_copy(u_send.at[most], u_recv.at[most], recv7).wait()
    for i in range(ns):
        u_ref[i : i + 1, :] = u_recv[i]
    flux_send[0] = jnp.sum(u_ref[...], axis=0, keepdims=True)

    def send_flux(step, carry):
        other = lax.rem(q + step, nf)
        pltpu.make_async_remote_copy(
            src_ref=flux_send, dst_ref=flux_recv.at[pl.ds(q, 1)], send_sem=send8, recv_sem=recv8,
            device_id={"freq": other}, device_id_type=MESH,
        ).start()
        return carry

    lax.fori_loop(1, nf, send_flux, 0)
    flux_recv[q] = flux_send[0]
    others = pl.ds(0, nf - 1)

    pltpu.make_async_copy(source_send.at[most], source_recv.at[most], send1).wait()
    pltpu.make_async_copy(vis_send.at[most], vis_recv.at[most], send3).wait()
    pltpu.make_async_copy(cot_send.at[most], cot_recv.at[most], send6).wait()
    pltpu.make_async_copy(u_send.at[most], u_recv.at[most], send7).wait()

    @pl.when(q == centre)
    def _():
        pltpu.make_async_copy(cot_all.at[others], cot_all.at[others], send5).wait()

    @pl.when(q != centre)
    def _():
        pltpu.make_async_copy(data_ref, dat_recv.at[0], send2).wait()
        pltpu.make_async_copy(vis_rows, vis_rows, send4).wait()

    pltpu.make_async_copy(flux_recv.at[others], flux_recv.at[others], recv8).wait()
    total = flux_recv[0]
    for i in range(1, nf):
        total = total + flux_recv[i]
    total_ref[...] = total
    pltpu.make_async_copy(flux_recv.at[others], flux_recv.at[others], send8).wait()


def body(source_dirs, flux, beam, counts, antennas, pairs, data, delay_weight):
    ns, nf = lax.axis_size("src"), lax.axis_size("freq")
    slots = flux.shape[0]
    nch = ns * nf
    share = LANES // nf
    rows = 2 * ns
    vmem, hbm = pl.BlockSpec(memory_space=pltpu.VMEM), pl.BlockSpec(memory_space=pltpu.HBM)
    dma = pltpu.SemaphoreType.DMA
    macs = 4 * ns * slots * 256 * 256
    tables = jnp.asarray(delay_tables(nch))
    inputs = (
        source_dirs, flux[None, :], beam, counts, antennas, pairs, jnp.transpose(data, (0, 2, 1)),
        delay_weight[None, :], tables,
    )
    gradient, total = pl.pallas_call(
        functools.partial(kernel, ns, nf, min(3, nf - 1)),
        out_shape=(
            jax.ShapeDtypeStruct((ns, slots), F32),
            jax.ShapeDtypeStruct((1, slots), F32),
        ),
        in_specs=[hbm] * len(inputs),
        out_specs=(vmem, vmem),
        scratch_shapes=[
            (pltpu.SMEM if i == 3 else pltpu.VMEM)(value.shape, value.dtype) for i, value in enumerate(inputs)
        ] + [
            pltpu.VMEM((ns, 4, slots), F32),
            pltpu.VMEM((ns, 4, slots), F32),
            pltpu.VMEM((ns, 2 * LANES, slots), BF16),
            pltpu.VMEM((ns, 2 * LANES, slots), BF16),
            pltpu.VMEM((2 * LANES, ns * LANES), BF16),
            pltpu.VMEM((LANES, ns * LANES), BF16),
            pltpu.VMEM((LANES, LANES), BF16),
            pltpu.VMEM((2 * LANES, slots), BF16),
            pltpu.VMEM((2 * LANES, slots), BF16),
            pltpu.VMEM((2 * LANES, slots), BF16),
            pltpu.VMEM((2 * LANES, slots), BF16),
            pltpu.VMEM((2 * LANES, 2 * LANES), F32),
            pltpu.VMEM((2 * LANES, 2 * LANES), F32),
            pltpu.VMEM((ns, 2, LANES), F32),
            pltpu.VMEM((ns, 2, LANES), F32),
            pltpu.VMEM((rows, LANES), F32),
            pltpu.VMEM((nf, rows, LANES), F32),
            pltpu.VMEM((nf, 2, share, nch), F32),
            pltpu.VMEM((2, 2 * nch, 2 * nch), BF16),
            pltpu.VMEM((2, 2 * nch, 2 * nch), BF16),
            pltpu.VMEM((nf, rows, LANES), F32),
            pltpu.VMEM((rows, LANES), F32),
            pltpu.VMEM((ns, 2, LANES), F32),
            pltpu.VMEM((ns, 2, LANES), F32),
            pltpu.VMEM((ns, 1, slots), F32),
            pltpu.VMEM((ns, 1, slots), F32),
            pltpu.VMEM((1, 1, slots), F32),
            pltpu.VMEM((nf, 1, slots), F32),
            dma((len(inputs),)),
            dma, dma((ns,)),
            dma, dma((nf,)),
            dma, dma,
            dma, dma((nf,)),
            dma, dma,
            dma, dma((ns // 4,)),
            dma, dma,
            dma, dma,
        ],
        compiler_params=pltpu.CompilerParams(
            collective_id=0, has_side_effects=True, vmem_limit_bytes=63 * 1024 * 1024
        ),
        cost_estimate=pl.CostEstimate(flops=2 * macs, bytes_accessed=4 * 1024 * 1024, transcendentals=0),
    )(*inputs)
    return (total[0] / flux, 2.0 * gradient / beam)


def solution(mesh):
    in_specs = (
        P(None, "src"),
        P("src"),
        P("freq", "src"),
        P(),
        P(),
        P(),
        P(None, None, ("src", "freq")),
        P(),
    )
    out_specs = (P("src"), P("freq", "src"))
    return jax.shard_map(body, mesh=mesh, in_specs=in_specs, out_specs=out_specs, check_vma=False)
```

time: 96.7 us -> 75.3 us (0.78)
  Pallas kernels: 87.1 us -> 71.8 us
  local copies, waits for them, and re-layouts: 7.32 us -> 0.01 us
  other arithmetic: 1.23 us -> 2.75 us
    pallas_call x1, Pallas kernels: 87.1 us -> 71.8 us  [body(): pl.pallas_call(functools.partial(kernel, ns, nf, min(3, nf - 1)), out_sha...]
    unnamed x18 -> x4, local copies, waits for them, and re-layouts: 7.32 us -> 0.01 us
    div x2, other arithmetic: 1.23 us -> 2.75 us  [body(): return (total[0] / flux, 2.0 * gradient / beam)]
where the time goes in v2:
time: 75.3 us; the launch traced here: 75.2 us
  Pallas kernels  71.8 us (95%)
  other arithmetic  2.75 us (4%)
    pallas_call x1, Pallas kernels, body(): pl.pallas_call(functools.partial(kernel, ns, nf, min(3, nf - 1)), out_sha...  71.8 us
    div x2, other arithmetic, body(): return (total[0] / flux, 2.0 * gradient / beam)  2.75 us

profile of v2, /device:TPU:1, one launch (start us, length us, event | category | flops | bytes accessed | tf_op | source)
XLA Modules:
  0.0 75.2 jit_solution(2509272549288276963)
XLA Ops:
  0.6 0.0 copy-start.1
  0.6 0.0 copy-start
  0.7 71.8 %shard_map.104 = (f32[32,512]{1,0:T(8,128)}, f32[1,512]{1,0:T(1,128)}) custom-call(f32[2,512]{1,0:T(2,128)} %dirs_hbm.1, f32[1,512]{1,0:T(1,128)} %bitcast.4, f32[32,512]{1,0:T(8,128)} %beam_hbm.1, s32[32]{0:T(128)} %counts_hbm.1, f32[3,128]{1,0:T(4,128)} %ant_hbm.1, s32[2,4096]{1,0:T(2,128)} %pairs_hbm.1, f32[2,16,256]{2,1,0:T(8,128)} %bitcast.6, ...), custom_call_target="tpu_custom_call" | custom-call | flops 8589934592 | bytes 4194304 | tf_op jit(solution)/shard_map/pallas_call | solution.py:479
  72.4 0.0 copy-done.1
  72.4 1.3 %div.6 = f32[512]{0:T(512)} divide(f32[512]{0:T(512)} %bitcast.5, f32[512]{0:T(512)S(1)} %copy-done.1) | non-fusion elementwise | flops 512 | bytes 6144 | tf_op jit(solution)/shard_map/div | solution.py:533
  73.7 0.0 copy-done
  73.7 1.5 %multiply_divide_fusion = f32[32,512]{1,0:T(8,128)} fusion(f32[32,512]{1,0:T(8,128)S(1)} %copy-done, f32[32,512]{1,0:T(8,128)} %get-tuple-element.5), kind=kLoop, calls=%fused_computation | loop fusion | flops 32768 | bytes 196608 | tf_op jit(solution)/shard_map/div | solution.py:533
Async XLA Ops:
  0.6 71.8 %copy-start.1 = (f32[512]{0:T(512)S(1)}, f32[512]{0:T(512)}, u32[]{:S(2)}) copy-start(f32[512]{0:T(512)} %param.10) | copy-start | bytes 6148
  0.6 73.1 %copy-start = (f32[32,512]{1,0:T(8,128)S(1)}, f32[32,512]{1,0:T(8,128)}, u32[]{:S(2)}) copy-start(f32[32,512]{1,0:T(8,128)} %beam_hbm.1) | copy-start | bytes 196612

commit v3 on v2

--- a/solution.py
+++ b/solution.py
@@ -16,7 +16,7 @@
 LANES = 128
 NT = (((1,), (1,)), ((), ()))
 NN = (((1,), (0,)), ((), ()))
-SIN_POLY = (3.141592640130707, -5.167710083507862, 2.550077523214134, -0.5982912856178576, 0.0776576603009221)
+SIN_POLY = (3.1415902702069913, -5.167406733272317, 2.544010518503151, -0.5594624554674011)
 COS_POLY = (0.9999999532476082, -4.93479283061961, 4.058411352862035, -1.3318765680776314, 0.2196896110917421)
 
 
@@ -89,7 +89,7 @@
     dirs_hbm, flux_hbm, beam_hbm, counts_hbm, ant_hbm, pairs_hbm, data_hbm, dw_hbm, tables_hbm,
     u_ref, total_ref,
     dirs_ref, flux_ref, beam_ref, counts_ref, ant_ref, pairs_ref, data_ref, dw_ref, tables,
-    source_send, source_recv, phased_hi, phased_lo, left_twice, one_right, ant_parts, even_hi, even_lo, odd_hi, odd_lo, gram_hh, gram_hl,
+    source_send, source_recv, phased_hi, phased_lo, phased_sum, left_twice, one_right, ant_parts, even_hi, even_lo, odd_hi, odd_lo, gram_hh, gram_hl,
     vis_send, vis_recv, vis_rows, vis_all, dat_recv, tables_hi, tables_lo, cot_all, cot_rows, cot_send, cot_recv,
     u_send, u_recv, flux_send, flux_recv,
     input_sem, send1, recv1, send2, recv2, send3, recv3, send4, recv4, send5, recv5, send6, recv6, send7, recv7,
@@ -173,7 +173,8 @@
         gram_hh[...] += dot(high, high, NT)
         gram_hl[...] += dot(high, low_ref[...], NT)
 
-    expand(s, even_hi, even_lo)
+    odd_hi[...] = jnp.zeros_like(odd_hi)
+    odd_lo[...] = jnp.zeros_like(odd_lo)
 
     antenna_id = lax.broadcasted_iota(jnp.int32, (LANES, 512), 0)
 
@@ -205,7 +206,7 @@
     def send_sources(step, carry):
         peer = peer_at(s, ns - step, ns)
         pltpu.make_async_remote_copy(
-            src_ref=source_send.at[peer], dst_ref=source_recv.at[s], send_sem=send1, recv_sem=recv1.at[s],
+            src_ref=source_send.at[peer], dst_ref=source_recv.at[s], send_sem=send1, recv_sem=recv1.at[s // 4],
             device_id={"src": peer}, device_id_type=MESH,
         ).start()
         return carry
@@ -223,26 +224,30 @@
             device_id={"freq": centre}, device_id_type=MESH,
         ).start()
 
-    def arrival(step):
-        k = peer_at(s, step, ns)
-        pltpu.make_async_remote_copy(
-            src_ref=source_send.at[k], dst_ref=source_recv.at[k], send_sem=send1, recv_sem=recv1.at[k],
-            device_id={"src": k}, device_id_type=MESH,
-        ).wait_recv()
-        return k
-
-    def forward(pair, carry):
-        k = arrival(2 * pair + 1)
-        later = arrival(2 * pair + 2)
-        expand(k, odd_hi, odd_lo)
+    def forward(step, carry):
+        j = quad_at(s // 4, step, ns // 4)
+
+        @pl.when(step == 0)
+        def _():
+            at = pl.ds(0, 3)
+            pltpu.make_async_copy(source_send.at[at], source_recv.at[at], recv1.at[j]).wait()
+
+        @pl.when(step != 0)
+        def _():
+            at = pl.ds(0, 4)
+            pltpu.make_async_copy(source_send.at[at], source_recv.at[at], recv1.at[j]).wait()
+
+        expand(j * 4, even_hi, even_lo)
+        correlate(odd_hi, odd_lo)
+        expand(j * 4 + 1, odd_hi, odd_lo)
         correlate(even_hi, even_lo)
-        expand(later, even_hi, even_lo)
+        expand(j * 4 + 2, even_hi, even_lo)
         correlate(odd_hi, odd_lo)
-        return carry
-
-    lax.fori_loop(0, ns // 2 - 1, forward, 0)
-    expand(arrival(ns - 1), odd_hi, odd_lo)
-    correlate(even_hi, even_lo)
+        expand(j * 4 + 3, odd_hi, odd_lo)
+        correlate(even_hi, even_lo)
+        return carry
+
+    lax.fori_loop(0, ns // 4, forward, 0)
     correlate(odd_hi, odd_lo)
 
     gram = gram_hh[...] + 2.0 * gram_hl[...]
@@ -289,6 +294,13 @@
 
         lax.fori_loop(1, nf, take_data, 0)
 
+    def add_parts(k, carry):
+        for top in range(0, 2 * LANES, 64):
+            at = pl.ds(top, 64)
+            phased_sum[k, at, :] = phased_hi[k, at, :].astype(F32) + 2.0 * phased_lo[k, at, :].astype(F32)
+        return carry
+
+    lax.fori_loop(0, ns, add_parts, 0)
     most = pl.ds(0, ns - 1)
     pltpu.make_async_copy(vis_send.at[most], vis_recv.at[most], recv3).wait()
     for i in range(ns):
@@ -392,36 +404,33 @@
     matrix = jnp.concatenate(
         [jnp.concatenate([real, -imag], axis=1), jnp.concatenate([imag, real], axis=1)], axis=0
     )
-    matrix_hi, matrix_lo = split(matrix)
+    matrix_parts = jnp.concatenate(split(matrix), axis=0)
 
     def pull_back(k):
         for lane in range(0, slots, 256):
             at = pl.ds(lane, 256)
             high = phased_hi[k, :, at]
-            product = dot(matrix_hi, high) + dot(matrix_lo, high)
-            phased = high.astype(F32) + 2.0 * phased_lo[k, :, at].astype(F32)
-            u_send[k, :, at] = jnp.sum(phased * product, axis=0, keepdims=True)
-
-    def send_gradient(k):
-        pltpu.make_async_remote_copy(
-            src_ref=u_send.at[k], dst_ref=u_recv.at[s], send_sem=send7, recv_sem=recv7,
-            device_id={"src": k}, device_id_type=MESH,
-        ).start()
-
-    def backward(pair, carry):
-        k = peer_at(s, ns - 1 - 2 * pair, ns)
-        later = peer_at(s, ns - 2 - 2 * pair, ns)
-        pull_back(k)
-        pull_back(later)
-        send_gradient(k)
-        send_gradient(later)
-        return carry
-
-    lax.fori_loop(0, ns // 2 - 1, backward, 0)
-    k = peer_at(s, 1, ns)
-    pull_back(k)
-    send_gradient(k)
-    pull_back(s)
+            product = dot(matrix_parts, high)
+            product = product[: 2 * LANES] + product[2 * LANES :]
+            u_send[k, :, at] = jnp.sum(phased_sum[k, :, at] * product, axis=0, keepdims=True)
+
+    def backward(step, carry):
+        j = quad_at(s // 4, ns // 4 - 1 - step, ns // 4)
+        for i in range(4):
+            pull_back(j * 4 + i)
+        for i in range(4):
+            peer = j * 4 + i
+
+            @pl.when(peer != s)
+            def _():
+                pltpu.make_async_remote_copy(
+                    src_ref=u_send.at[peer], dst_ref=u_recv.at[s], send_sem=send7, recv_sem=recv7,
+                    device_id={"src": peer}, device_id_type=MESH,
+                ).start()
+
+        return carry
+
+    lax.fori_loop(0, ns // 4, backward, 0)
     u_recv[s] = u_send[s]
     pltpu.make_async_copy(u_send.at[most], u_recv.at[most], recv7).wait()
     for i in range(ns):
@@ -479,8 +488,8 @@
     gradient, total = pl.pallas_call(
         functools.partial(kernel, ns, nf, min(3, nf - 1)),
         out_shape=(
-            jax.ShapeDtypeStruct((ns, slots), F32),
-            jax.ShapeDtypeStruct((1, slots), F32),
+            pltpu.VMEM((ns, slots), F32),
+            pltpu.VMEM((1, slots), F32),
         ),
         in_specs=[hbm] * len(inputs),
         out_specs=(vmem, vmem),
@@ -491,6 +500,7 @@
             pltpu.VMEM((ns, 4, slots), F32),
             pltpu.VMEM((ns, 2 * LANES, slots), BF16),
             pltpu.VMEM((ns, 2 * LANES, slots), BF16),
+            pltpu.VMEM((ns, 2 * LANES, slots), F32),
             pltpu.VMEM((2 * LANES, ns * LANES), BF16),
             pltpu.VMEM((LANES, ns * LANES), BF16),
             pltpu.VMEM((LANES, LANES), BF16),
@@ -516,7 +526,7 @@
             pltpu.VMEM((1, 1, slots), F32),
             pltpu.VMEM((nf, 1, slots), F32),
             dma((len(inputs),)),
-            dma, dma((ns,)),
+            dma, dma((ns // 4,)),
             dma, dma((nf,)),
             dma, dma,
             dma, dma((nf,)),

time: 75.3 us -> 69.8 us (0.927)
  Pallas kernels: 71.8 us -> 67.8 us
  other arithmetic: 2.75 us -> 1.23 us
    pallas_call x1, Pallas kernels: 71.8 us -> 67.8 us  [body(): pl.pallas_call(functools.partial(kernel, ns, nf, min(3, nf - 1)), out_sha...]
    div x2, other arithmetic: 2.75 us -> 1.23 us  [body(): return (total[0] / flux, 2.0 * gradient / beam)]
where the time goes in v3:
time: 69.8 us; the launch traced here: 69.7 us
  Pallas kernels  67.8 us (97%)
  other arithmetic  1.23 us (2%)
    pallas_call x1, Pallas kernels, body(): pl.pallas_call(functools.partial(kernel, ns, nf, min(3, nf - 1)), out_sha...  67.8 us

profile of v3, /device:TPU:1, one launch (start us, length us, event | category | flops | bytes accessed | tf_op | source)
XLA Modules:
  0.0 69.7 jit_solution(10852633192526849242)
XLA Ops:
  0.6 0.0 copy-start.1
  0.6 0.0 copy-start
  0.7 67.8 %shard_map.104 = (f32[32,512]{1,0:T(8,128)S(1)}, f32[1,512]{1,0:T(1,128)S(1)}) custom-call(f32[2,512]{1,0:T(2,128)} %dirs_hbm.1, f32[1,512]{1,0:T(1,128)} %bitcast.5, f32[32,512]{1,0:T(8,128)} %beam_hbm.1, s32[32]{0:T(128)} %counts_hbm.1, f32[3,128]{1,0:T(4,128)} %ant_hbm.1, s32[2,4096]{1,0:T(2,128)} %pairs_hbm.1, f32[2,16,256]{2,1,0:T(8,128)} %bitcast.6, ...), custom_call_target="tpu_custom_call" | custom-call | flops 8589934592 | bytes 4194304 | tf_op jit(solution)/shard_map/pallas_call | solution.py:488
  68.5 0.0 copy-done.1
  68.5 0.6 div.6
  69.1 0.0 copy-done
  69.1 0.6 multiply_divide_fusion
Async XLA Ops:
  0.6 67.8 %copy-start.1 = (f32[512]{0:T(512)S(1)}, f32[512]{0:T(512)}, u32[]{:S(2)}) copy-start(f32[512]{0:T(512)} %param.10) | copy-start | bytes 6148
  0.6 68.4 %copy-start = (f32[32,512]{1,0:T(8,128)S(1)}, f32[32,512]{1,0:T(8,128)}, u32[]{:S(2)}) copy-start(f32[32,512]{1,0:T(8,128)} %beam_hbm.1) | copy-start | bytes 196612

commit v4 on v3

--- a/solution.py
+++ b/solution.py
@@ -90,15 +90,15 @@
     u_ref, total_ref,
     dirs_ref, flux_ref, beam_ref, counts_ref, ant_ref, pairs_ref, data_ref, dw_ref, tables,
     source_send, source_recv, phased_hi, phased_lo, phased_sum, left_twice, one_right, ant_parts, even_hi, even_lo, odd_hi, odd_lo, gram_hh, gram_hl,
-    vis_send, vis_recv, vis_rows, vis_all, dat_recv, tables_hi, tables_lo, cot_all, cot_rows, cot_send, cot_recv,
+    vis_send, vis_all, vis_rows, dat_recv, tables_hi, tables_lo, cot_all, cot_recv,
     u_send, u_recv, flux_send, flux_recv,
-    input_sem, send1, recv1, send2, recv2, send3, recv3, send4, recv4, send5, recv5, send6, recv6, send7, recv7,
+    input_sem, send1, recv1, send2, recv2, send3, recv3, send6, recv6, send7, recv7,
     send8, recv8,
 ):
     nch = ns * nf
     slots = dirs_ref.shape[1]
     nb = ns * LANES
-    rows = 2 * ns
+    quads = ns // 4
     s = lax.axis_index("src")
     q = lax.axis_index("freq")
 
@@ -114,15 +114,35 @@
         copy.start()
     barrier = pltpu.get_barrier_semaphore()
 
-    def greet_src(step, carry):
-        pl.semaphore_signal(barrier, inc=1, device_id={"src": peer_at(s, ns - step, ns)}, device_id_type=MESH)
+    def greet(peer, group):
+        pl.semaphore_signal(barrier, inc=1, device_id={"src": peer, "freq": group}, device_id_type=MESH)
+
+    def greet_quad(step, carry):
+        j = quad_at(s // 4, quads - 1 - step, quads)
+        for i in range(4):
+            peer = j * 4 + i
+
+            @pl.when(peer != s)
+            def _():
+                greet(peer, q)
+
+                @pl.when(q != centre)
+                def _():
+                    greet(peer, centre)
+
+                @pl.when(q == centre)
+                def _():
+                    for group in range(nf):
+                        if group != centre:
+                            greet(peer, group)
+
         return carry
 
     def greet_freq(step, carry):
-        pl.semaphore_signal(barrier, inc=1, device_id={"freq": lax.rem(q + step, nf)}, device_id_type=MESH)
-        return carry
-
-    lax.fori_loop(1, ns, greet_src, 0)
+        greet(s, lax.rem(q + step, nf))
+        return carry
+
+    lax.fori_loop(0, quads, greet_quad, 0)
     lax.fori_loop(1, nf, greet_freq, 0)
     for copy in inputs[:8]:
         copy.wait()
@@ -201,17 +221,30 @@
 
         lax.fori_loop(0, 2 * nch // piece, split_tables, 0)
 
-    pl.semaphore_wait(barrier, ns - 1 + nf - 1)
+    @pl.when(q == centre)
+    def _():
+        pl.semaphore_wait(barrier, nch - 1)
+
+    @pl.when(q != centre)
+    def _():
+        pl.semaphore_wait(barrier, 2 * (ns - 1) + nf - 1)
+
 
     def send_sources(step, carry):
-        peer = peer_at(s, ns - step, ns)
-        pltpu.make_async_remote_copy(
-            src_ref=source_send.at[peer], dst_ref=source_recv.at[s], send_sem=send1, recv_sem=recv1.at[s // 4],
-            device_id={"src": peer}, device_id_type=MESH,
-        ).start()
-        return carry
-
-    lax.fori_loop(1, ns, send_sources, 0)
+        j = quad_at(s // 4, step, quads)
+        for i in range(4):
+            peer = j * 4 + i
+
+            @pl.when(peer != s)
+            def _():
+                pltpu.make_async_remote_copy(
+                    src_ref=source_send.at[peer], dst_ref=source_recv.at[s], send_sem=send1,
+                    recv_sem=recv1.at[s // 4], device_id={"src": peer}, device_id_type=MESH,
+                ).start()
+
+        return carry
+
+    lax.fori_loop(0, quads, send_sources, 0)
 
     @pl.when(q == centre)
     def _():
@@ -225,7 +258,7 @@
         ).start()
 
     def forward(step, carry):
-        j = quad_at(s // 4, step, ns // 4)
+        j = quad_at(s // 4, step, quads)
 
         @pl.when(step == 0)
         def _():
@@ -247,7 +280,7 @@
         correlate(even_hi, even_lo)
         return carry
 
-    lax.fori_loop(0, ns // 4, forward, 0)
+    lax.fori_loop(0, quads, forward, 0)
     correlate(odd_hi, odd_lo)
 
     gram = gram_hh[...] + 2.0 * gram_hl[...]
@@ -259,7 +292,7 @@
     grid_parts = jnp.concatenate([grid_hi, grid_lo], axis=1)
 
     def gather(step, carry):
-        j = quad_at(s // 4, ns // 4 - 1 - step, ns // 4)
+        j = quad_at(s // 4, quads - 1 - step, quads)
         at = pl.ds(pl.multiple_of(j * 512, 512), 512)
         picked = dot(grid_parts, left_twice[:, at])
         right = one_right[:, at].astype(F32)
@@ -270,17 +303,27 @@
             vis_send[peer, 0:1, :] = real[:, i * LANES : (i + 1) * LANES]
             vis_send[peer, 1:2, :] = imag[:, i * LANES : (i + 1) * LANES]
 
-            @pl.when(peer != s)
+            @pl.when(jnp.logical_or(peer != s, q != centre))
             def _():
                 pltpu.make_async_remote_copy(
-                    src_ref=vis_send.at[peer], dst_ref=vis_recv.at[s], send_sem=send3, recv_sem=recv3,
-                    device_id={"src": peer}, device_id_type=MESH,
+                    src_ref=vis_send.at[peer], dst_ref=vis_all.at[q * ns + s], send_sem=send3, recv_sem=recv3,
+                    device_id={"src": peer, "freq": centre}, device_id_type=MESH,
                 ).start()
 
         return carry
 
-    lax.fori_loop(0, ns // 4, gather, 0)
-    vis_recv[s] = vis_send[s]
+    lax.fori_loop(0, quads, gather, 0)
+
+    def add_parts(k, carry):
+        for top in range(0, 2 * LANES, 64):
+            at = pl.ds(top, 64)
+            phased_sum[k, at, :] = phased_hi[k, at, :].astype(F32) + 2.0 * phased_lo[k, at, :].astype(F32)
+        return carry
+
+    lax.fori_loop(0, ns, add_parts, 0)
+    most = pl.ds(0, ns - 1)
+    others = pl.ds(0, nf - 1)
+    all_but_one = pl.ds(0, nch - 1)
 
     @pl.when(q == centre)
     def _():
@@ -294,29 +337,6 @@
 
         lax.fori_loop(1, nf, take_data, 0)
 
-    def add_parts(k, carry):
-        for top in range(0, 2 * LANES, 64):
-            at = pl.ds(top, 64)
-            phased_sum[k, at, :] = phased_hi[k, at, :].astype(F32) + 2.0 * phased_lo[k, at, :].astype(F32)
-        return carry
-
-    lax.fori_loop(0, ns, add_parts, 0)
-    most = pl.ds(0, ns - 1)
-    pltpu.make_async_copy(vis_send.at[most], vis_recv.at[most], recv3).wait()
-    for i in range(ns):
-        vis_rows[2 * i : 2 * i + 2, :] = vis_recv[i]
-
-    @pl.when(q != centre)
-    def _():
-        pltpu.make_async_remote_copy(
-            src_ref=vis_rows, dst_ref=vis_all.at[q], send_sem=send4, recv_sem=recv4.at[q],
-            device_id={"freq": centre}, device_id_type=MESH,
-        ).start()
-
-    @pl.when(q == centre)
-    def _():
-        vis_all[q] = vis_rows[...]
-
         def three_passes(i, high, low):
             both = dot(tables_hi[i], jnp.concatenate([high, low], axis=1))
             return both[:, :LANES] + both[:, LANES:] + dot(tables_lo[i], high)
@@ -325,68 +345,60 @@
         spectra = [
             jnp.transpose(jnp.concatenate([dat_recv[i, c] for i in range(nf)], axis=0)) for c in range(2)
         ]
-
-        def take_vis(step, carry):
-            other = lax.rem(q + step, nf)
-            pltpu.make_async_remote_copy(
-                src_ref=vis_rows, dst_ref=vis_all.at[other], send_sem=send4, recv_sem=recv4.at[other],
-                device_id={"freq": other}, device_id_type=MESH,
-            ).wait_recv()
+        vis_all[q * ns + s] = vis_send[s]
+        pltpu.make_async_copy(vis_all.at[all_but_one], vis_all.at[all_but_one], recv3).wait()
+
+        def pack(j, carry):
+            at = pl.ds(pl.multiple_of(j * 16, 16), 16)
+            vis_rows[at, :] = jnp.concatenate([vis_all[j * 8 + i] for i in range(8)], axis=0)
             return carry
 
-        lax.fori_loop(1, nf, take_vis, 0)
-        vis_hi, vis_lo = split(jnp.concatenate([vis_all[i] for i in range(nf)], axis=0))
+        lax.fori_loop(0, nch // 8, pack, 0)
+        vis_hi, vis_lo = split(vis_rows[...])
         spec = three_passes(0, vis_hi, vis_lo)
         spec_cot = jnp.concatenate(
             [weight * (spec[:nch] - spectra[0]), weight * (spec[nch:] - spectra[1])], axis=0
         )
         cot_hi, cot_lo = split(spec_cot)
-        back = three_passes(1, cot_hi, cot_lo)
-        for i in range(nf):
-            cot_all[i] = back[i * rows : (i + 1) * rows]
+        vis_rows[...] = three_passes(1, cot_hi, cot_lo)
 
         def send_cot(step, carry):
-            other = lax.rem(q + step, nf)
-            pltpu.make_async_remote_copy(
-                src_ref=cot_all.at[other], dst_ref=cot_rows, send_sem=send5, recv_sem=recv5,
-                device_id={"freq": other}, device_id_type=MESH,
-            ).start()
+            j = quad_at(s // 4, quads - 1 - step, quads)
+            for group in range(nf):
+                first = group * ns + j * 4
+                piece = vis_rows[pl.ds(pl.multiple_of(first * 2, 8), 8), :]
+                for i in range(4):
+                    peer = j * 4 + i
+                    cot_all[first + i] = piece[2 * i : 2 * i + 2]
+
+                    def send():
+                        pltpu.make_async_remote_copy(
+                            src_ref=cot_all.at[first + i], dst_ref=cot_recv.at[s], send_sem=send6,
+                            recv_sem=recv6.at[s // 4], device_id={"src": peer, "freq": group},
+                            device_id_type=MESH,
+                        ).start()
+
+                    if group == centre:
+                        pl.when(peer != s)(send)
+                    else:
+                        send()
             return carry
 
-        lax.fori_loop(1, nf, send_cot, 0)
-        cot_rows[...] = cot_all[q]
-
-    @pl.when(q != centre)
-    def _():
-        pltpu.make_async_remote_copy(
-            src_ref=cot_all.at[q], dst_ref=cot_rows, send_sem=send5, recv_sem=recv5,
-            device_id={"freq": centre}, device_id_type=MESH,
-        ).wait_recv()
-
-    for i in range(ns):
-        cot_send[i] = cot_rows[2 * i : 2 * i + 2, :]
-
-    def fan_out(step, carry):
-        peer = peer_at(s, ns - step, ns)
-        pltpu.make_async_remote_copy(
-            src_ref=cot_send.at[peer], dst_ref=cot_recv.at[s], send_sem=send6, recv_sem=recv6.at[s // 4],
-            device_id={"src": peer}, device_id_type=MESH,
-        ).start()
-        return carry
-
-    lax.fori_loop(1, ns, fan_out, 0)
-    cot_recv[s] = cot_send[s]
+        lax.fori_loop(0, quads, send_cot, 0)
+        cot_recv[s] = cot_all[q * ns + s]
 
     def scatter(step, total):
-        j = quad_at(s // 4, step, ns // 4)
-
-        @pl.when(step == 0)
+        j = quad_at(s // 4, step, quads)
+
+        with_own = jnp.logical_and(step == 0, q == centre)
+
+        @pl.when(with_own)
         def _():
-            pltpu.make_async_copy(cot_send.at[pl.ds(0, 3)], cot_recv.at[pl.ds(0, 3)], recv6.at[j]).wait()
-
-        @pl.when(step != 0)
+            pltpu.make_async_copy(cot_recv.at[pl.ds(0, 3)], cot_recv.at[pl.ds(0, 3)], recv6.at[j]).wait()
+
+        @pl.when(jnp.logical_not(with_own))
         def _():
-            pltpu.make_async_copy(cot_send.at[pl.ds(0, 4)], cot_recv.at[pl.ds(0, 4)], recv6.at[j]).wait()
+            pltpu.make_async_copy(cot_recv.at[pl.ds(0, 4)], cot_recv.at[pl.ds(0, 4)], recv6.at[j]).wait()
 
         at = pl.ds(pl.multiple_of(j * 512, 512), 512)
         right = one_right[:, at]
@@ -397,7 +409,7 @@
         scaled = [right * parts[c][part] for part in range(2) for c in range(2)]
         return total + dot(left_twice[:LANES, at], jnp.concatenate(scaled, axis=0), NT)
 
-    grids = lax.fori_loop(0, ns // 4, scatter, jnp.zeros((LANES, 4 * LANES), F32))
+    grids = lax.fori_loop(0, quads, scatter, jnp.zeros((LANES, 4 * LANES), F32))
     grids = grids[:, : 2 * LANES] + grids[:, 2 * LANES :]
     real, imag = grids[:, :LANES], grids[:, LANES:]
     real, imag = 0.5 * (real + real.T), 0.5 * (imag - imag.T)
@@ -415,7 +427,7 @@
             u_send[k, :, at] = jnp.sum(phased_sum[k, :, at] * product, axis=0, keepdims=True)
 
     def backward(step, carry):
-        j = quad_at(s // 4, ns // 4 - 1 - step, ns // 4)
+        j = quad_at(s // 4, quads - 1 - step, quads)
         for i in range(4):
             pull_back(j * 4 + i)
         for i in range(4):
@@ -430,7 +442,7 @@
 
         return carry
 
-    lax.fori_loop(0, ns // 4, backward, 0)
+    lax.fori_loop(0, quads, backward, 0)
     u_recv[s] = u_send[s]
     pltpu.make_async_copy(u_send.at[most], u_recv.at[most], recv7).wait()
     for i in range(ns):
@@ -447,21 +459,18 @@
 
     lax.fori_loop(1, nf, send_flux, 0)
     flux_recv[q] = flux_send[0]
-    others = pl.ds(0, nf - 1)
-
     pltpu.make_async_copy(source_send.at[most], source_recv.at[most], send1).wait()
-    pltpu.make_async_copy(vis_send.at[most], vis_recv.at[most], send3).wait()
-    pltpu.make_async_copy(cot_send.at[most], cot_recv.at[most], send6).wait()
     pltpu.make_async_copy(u_send.at[most], u_recv.at[most], send7).wait()
 
     @pl.when(q == centre)
     def _():
-        pltpu.make_async_copy(cot_all.at[others], cot_all.at[others], send5).wait()
+        pltpu.make_async_copy(vis_send.at[most], vis_send.at[most], send3).wait()
+        pltpu.make_async_copy(cot_all.at[all_but_one], cot_all.at[all_but_one], send6).wait()
 
     @pl.when(q != centre)
     def _():
+        pltpu.make_async_copy(vis_send, vis_send, send3).wait()
         pltpu.make_async_copy(data_ref, dat_recv.at[0], send2).wait()
-        pltpu.make_async_copy(vis_rows, vis_rows, send4).wait()
 
     pltpu.make_async_copy(flux_recv.at[others], flux_recv.at[others], recv8).wait()
     total = flux_recv[0]
@@ -476,7 +485,6 @@
     slots = flux.shape[0]
     nch = ns * nf
     share = LANES // nf
-    rows = 2 * ns
     vmem, hbm = pl.BlockSpec(memory_space=pltpu.VMEM), pl.BlockSpec(memory_space=pltpu.HBM)
     dma = pltpu.SemaphoreType.DMA
     macs = 4 * ns * slots * 256 * 256
@@ -511,15 +519,12 @@
             pltpu.VMEM((2 * LANES, 2 * LANES), F32),
             pltpu.VMEM((2 * LANES, 2 * LANES), F32),
             pltpu.VMEM((ns, 2, LANES), F32),
-            pltpu.VMEM((ns, 2, LANES), F32),
-            pltpu.VMEM((rows, LANES), F32),
-            pltpu.VMEM((nf, rows, LANES), F32),
+            pltpu.VMEM((nch, 2, LANES), F32),
+            pltpu.VMEM((2 * nch, LANES), F32),
             pltpu.VMEM((nf, 2, share, nch), F32),
             pltpu.VMEM((2, 2 * nch, 2 * nch), BF16),
             pltpu.VMEM((2, 2 * nch, 2 * nch), BF16),
-            pltpu.VMEM((nf, rows, LANES), F32),
-            pltpu.VMEM((rows, LANES), F32),
-            pltpu.VMEM((ns, 2, LANES), F32),
+            pltpu.VMEM((nch, 2, LANES), F32),
             pltpu.VMEM((ns, 2, LANES), F32),
             pltpu.VMEM((ns, 1, slots), F32),
             pltpu.VMEM((ns, 1, slots), F32),
@@ -527,8 +532,6 @@
             pltpu.VMEM((nf, 1, slots), F32),
             dma((len(inputs),)),
             dma, dma((ns // 4,)),
-            dma, dma((nf,)),
-            dma, dma,
             dma, dma((nf,)),
             dma, dma,
             dma, dma((ns // 4,)),

time: 69.8 us -> 62.9 us (0.901)
  Pallas kernels: 67.8 us -> 60.9 us
    pallas_call x1, Pallas kernels: 67.8 us -> 60.9 us  [body(): pl.pallas_call(functools.partial(kernel, ns, nf, min(3, nf - 1)), out_sha...]
where the time goes in v4:
time: 62.9 us; the launch traced here: 62.8 us
  Pallas kernels  60.9 us (97%)
  other arithmetic  1.23 us (2%)
  between operations  0.67 us (1%)
    pallas_call x1, Pallas kernels, body(): pl.pallas_call(functools.partial(kernel, ns, nf, min(3, nf - 1)), out_sha...  60.9 us

profile of v4, /device:TPU:1, one launch (start us, length us, event | category | flops | bytes accessed | tf_op | source)
XLA Modules:
  0.0 62.8 jit_solution(1267780126622552702)
XLA Ops:
  0.6 0.0 copy-start.1
  0.6 0.0 copy-start
  0.7 60.9 %shard_map.104 = (f32[32,512]{1,0:T(8,128)S(1)}, f32[1,512]{1,0:T(1,128)S(1)}) custom-call(f32[2,512]{1,0:T(2,128)} %dirs_hbm.1, f32[1,512]{1,0:T(1,128)} %bitcast.5, f32[32,512]{1,0:T(8,128)} %beam_hbm.1, s32[32]{0:T(128)} %counts_hbm.1, f32[3,128]{1,0:T(4,128)} %ant_hbm.1, s32[2,4096]{1,0:T(2,128)} %pairs_hbm.1, f32[2,16,256]{2,1,0:T(8,128)} %bitcast.6, ...), custom_call_target="tpu_custom_call" | custom-call | flops 8589934592 | bytes 4194304 | tf_op jit(solution)/shard_map/pallas_call | solution.py:496
  61.6 0.0 copy-done.1
  61.6 0.6 div.6
  62.2 0.0 copy-done
  62.2 0.6 %multiply_divide_fusion = f32[32,512]{1,0:T(8,128)} fusion(f32[32,512]{1,0:T(8,128)S(1)} %copy-done, f32[32,512]{1,0:T(8,128)S(1)} %get-tuple-element.5), kind=kLoop, calls=%fused_computation | loop fusion | flops 32768 | bytes 196608 | tf_op jit(solution)/shard_map/div | solution.py:546
Async XLA Ops:
  0.6 61.0 %copy-start.1 = (f32[512]{0:T(512)S(1)}, f32[512]{0:T(512)}, u32[]{:S(2)}) copy-start(f32[512]{0:T(512)} %param.10) | copy-start | bytes 6148
  0.6 61.5 %copy-start = (f32[32,512]{1,0:T(8,128)S(1)}, f32[32,512]{1,0:T(8,128)}, u32[]{:S(2)}) copy-start(f32[32,512]{1,0:T(8,128)} %beam_hbm.1) | copy-start | bytes 196612

commit v5 on v4

--- a/solution.py
+++ b/solution.py
@@ -17,7 +17,7 @@
 NT = (((1,), (1,)), ((), ()))
 NN = (((1,), (0,)), ((), ()))
 SIN_POLY = (3.1415902702069913, -5.167406733272317, 2.544010518503151, -0.5594624554674011)
-COS_POLY = (0.9999999532476082, -4.93479283061961, 4.058411352862035, -1.3318765680776314, 0.2196896110917421)
+COS_POLY = (0.9999932488527381, -4.933934668076284, 4.041248101995494, -1.2220317625317256)
 
 
 def dot(left, right, dims=NN):
@@ -66,14 +66,8 @@
     return np.stack([forward, forward.T]).astype(np.float32)
 
 
-def peer_at(own, step, count):
-    if count != 32:
-        return lax.rem(own + step, count)
-    own_x, own_z, own_y = lax.rem(own, 4), lax.rem(own // 4, 2), own // 8
-    x = lax.rem(own_x + lax.rem(step, 4), 4)
-    y = lax.rem(own_y + lax.rem(step // 4, 4), 4)
-    z = lax.rem(own_z + step // 16, 2)
-    return y * 8 + z * 4 + x
+def in_quad(own, step):
+    return own // 4 * 4 + lax.rem(own + step, 4)
 
 
 def quad_at(own, step, count):
@@ -89,7 +83,7 @@
     dirs_hbm, flux_hbm, beam_hbm, counts_hbm, ant_hbm, pairs_hbm, data_hbm, dw_hbm, tables_hbm,
     u_ref, total_ref,
     dirs_ref, flux_ref, beam_ref, counts_ref, ant_ref, pairs_ref, data_ref, dw_ref, tables,
-    source_send, source_recv, phased_hi, phased_lo, phased_sum, left_twice, one_right, ant_parts, even_hi, even_lo, odd_hi, odd_lo, gram_hh, gram_hl,
+    source_send, source_recv, phased_hi, phased_lo, phased_sum, left_twice, one_right, ant_parts, even_hi, even_lo, odd_hi, odd_lo, gram_hh, gram_hl, grids_ref,
     vis_send, vis_all, vis_rows, dat_recv, tables_hi, tables_lo, cot_all, cot_recv,
     u_send, u_recv, flux_send, flux_recv,
     input_sem, send1, recv1, send2, recv2, send3, recv3, send6, recv6, send7, recv7,
@@ -147,39 +141,48 @@
     for copy in inputs[:8]:
         copy.wait()
 
-    along_l, along_m = dirs_ref[0:1, :], dirs_ref[1:2, :]
-    along_n = jnp.sqrt(1.0 - along_l * along_l - along_m * along_m)
     live = lax.broadcasted_iota(jnp.int32, (1, slots), 1) < counts_ref[s]
     strength = jnp.where(live, jnp.sqrt(flux_ref[...] * (1.0 / math.sqrt(slots * ns))), 0.0)
     roots = beam_ref[...] * strength
+    along = jnp.concatenate(
+        [dirs_ref[i : i + 1, pl.ds(j * LANES, LANES)] for i in range(2) for j in range(4)], axis=0
+    )
     for i in range(ns):
-        source_send[i, 0:1, :] = along_l
-        source_send[i, 1:2, :] = along_m
-        source_send[i, 2:3, :] = along_n
-        source_send[i, 3:4, :] = roots[i : i + 1, :]
+        source_send[i, 0:8, :] = along
+        for j in range(4):
+            source_send[i, 8 + j : 9 + j, :] = roots[i : i + 1, j * LANES : (j + 1) * LANES]
     source_recv[s] = source_send[s]
 
     freq = 1.0 + 0.6 * (q * ns + s).astype(F32) / nch
-    first, second, third = three_parts(
-        jnp.concatenate([ant_ref[...] * freq, jnp.zeros((5, LANES), F32)], axis=0)
+    positions = jnp.concatenate(
+        [jnp.broadcast_to(ant_ref[i : i + 1, :] * freq, (4, LANES)) for i in range(3)]
+        + [jnp.zeros((4, LANES), F32)],
+        axis=0,
     )
-    spare = jnp.zeros((LANES - 48, LANES), F32)
-    ant_parts[...] = jnp.transpose(
-        jnp.concatenate([first, second, third, first, second, first, spare], axis=0)
-    ).astype(BF16)
+    row = lax.broadcasted_iota(jnp.int32, (16, LANES), 0)
+    for j in range(4):
+        first, second, third = three_parts(jnp.where(row % 4 == j, positions, 0.0))
+        spare = jnp.zeros((LANES - 96, LANES), F32)
+        ant_parts[j * LANES : (j + 1) * LANES, :] = jnp.transpose(
+            jnp.concatenate([first, second, third, first, second, first, spare], axis=0)
+        ).astype(BF16)
 
     gram_hh[...] = jnp.zeros_like(gram_hh)
     gram_hl[...] = jnp.zeros_like(gram_hl)
 
     def expand(k, high_ref, low_ref):
-        source = jnp.concatenate([source_recv[k], jnp.zeros((4, slots), F32)], axis=0)
+        source = source_recv[k]
+        along_l, along_m = source[0:4], source[4:8]
+        along_n = jnp.sqrt(1.0 - along_l * along_l - along_m * along_m)
+        source = jnp.concatenate([along_l, along_m, along_n, jnp.zeros_like(along_n)], axis=0)
         first, second, third = three_parts(source)
         parts = jnp.concatenate([first, first, first, second, second, third], axis=0).astype(BF16)
-        turns = dot(ant_parts[:, :48], parts)
+        turns = dot(ant_parts[:, :96], parts)
         for lane in range(0, slots, LANES):
-            root = source_recv[k, 3:4, pl.ds(lane, LANES)]
+            piece = lane // LANES
+            root = source_recv[k, 8 + piece : 9 + piece, :]
             for top in range(0, LANES, 64):
-                cosine, sine = scaled_cos_sin(turns[top : top + 64, lane : lane + LANES], root)
+                cosine, sine = scaled_cos_sin(turns[lane + top : lane + top + 64], root)
                 for base, value in ((0, cosine), (LANES, sine)):
                     high, low = split(value)
                     at = (pl.ds(base + top, 64), pl.ds(lane, LANES))
@@ -291,28 +294,36 @@
     grid_hi, grid_lo = split(jnp.concatenate([vis_re, -vis_im], axis=0))
     grid_parts = jnp.concatenate([grid_hi, grid_lo], axis=1)
 
+    pair = min(2, quads)
+
     def gather(step, carry):
-        j = quad_at(s // 4, quads - 1 - step, quads)
-        at = pl.ds(pl.multiple_of(j * 512, 512), 512)
-        picked = dot(grid_parts, left_twice[:, at])
-        right = one_right[:, at].astype(F32)
-        real = jnp.sum(picked[:LANES] * right, axis=0, keepdims=True)
-        imag = jnp.sum(picked[LANES:] * right, axis=0, keepdims=True)
-        for i in range(4):
-            peer = j * 4 + i
-            vis_send[peer, 0:1, :] = real[:, i * LANES : (i + 1) * LANES]
-            vis_send[peer, 1:2, :] = imag[:, i * LANES : (i + 1) * LANES]
-
-            @pl.when(jnp.logical_or(peer != s, q != centre))
-            def _():
-                pltpu.make_async_remote_copy(
-                    src_ref=vis_send.at[peer], dst_ref=vis_all.at[q * ns + s], send_sem=send3, recv_sem=recv3,
-                    device_id={"src": peer, "freq": centre}, device_id_type=MESH,
-                ).start()
-
-        return carry
-
-    lax.fori_loop(0, quads, gather, 0)
+        chosen = [quad_at(s // 4, quads - 1 - step * pair - i, quads) for i in range(pair)]
+        rows = []
+        for j in chosen:
+            at = pl.ds(pl.multiple_of(j * 512, 512), 512)
+            picked = dot(grid_parts, left_twice[:, at])
+            right = one_right[:, at].astype(F32)
+            rows.append([
+                jnp.sum(picked[c * LANES : (c + 1) * LANES] * right, axis=0, keepdims=True) for c in range(2)
+            ])
+        for j, row in zip(chosen, rows):
+            for i in range(4):
+                for c in range(2):
+                    vis_send[j * 4 + i, c : c + 1, :] = row[c][:, i * LANES : (i + 1) * LANES]
+        for j in chosen:
+            for i in range(4):
+                peer = j * 4 + i
+
+                @pl.when(jnp.logical_or(peer != s, q != centre))
+                def _():
+                    pltpu.make_async_remote_copy(
+                        src_ref=vis_send.at[peer], dst_ref=vis_all.at[q * ns + s], send_sem=send3, recv_sem=recv3,
+                        device_id={"src": peer, "freq": centre}, device_id_type=MESH,
+                    ).start()
+
+        return carry
+
+    lax.fori_loop(0, quads // pair, gather, 0)
 
     def add_parts(k, carry):
         for top in range(0, 2 * LANES, 64):
@@ -387,29 +398,39 @@
         lax.fori_loop(0, quads, send_cot, 0)
         cot_recv[s] = cot_all[q * ns + s]
 
-    def scatter(step, total):
-        j = quad_at(s // 4, step, quads)
-
-        with_own = jnp.logical_and(step == 0, q == centre)
-
-        @pl.when(with_own)
-        def _():
-            pltpu.make_async_copy(cot_recv.at[pl.ds(0, 3)], cot_recv.at[pl.ds(0, 3)], recv6.at[j]).wait()
-
-        @pl.when(jnp.logical_not(with_own))
-        def _():
-            pltpu.make_async_copy(cot_recv.at[pl.ds(0, 4)], cot_recv.at[pl.ds(0, 4)], recv6.at[j]).wait()
-
-        at = pl.ds(pl.multiple_of(j * 512, 512), 512)
-        right = one_right[:, at]
-        parts = []
-        for c in range(2):
-            row = jnp.concatenate([cot_recv[j * 4 + i, c : c + 1, :] for i in range(4)], axis=1)
-            parts.append(split(row))
-        scaled = [right * parts[c][part] for part in range(2) for c in range(2)]
-        return total + dot(left_twice[:LANES, at], jnp.concatenate(scaled, axis=0), NT)
-
-    grids = lax.fori_loop(0, quads, scatter, jnp.zeros((LANES, 4 * LANES), F32))
+    many = min(4, quads)
+
+    def scatter(half, carry):
+        total = grids_ref[...]
+        for i in range(many):
+            step = half * many + i
+            j = quad_at(s // 4, step, quads)
+            with_own = jnp.logical_and(step == 0, q == centre)
+
+            @pl.when(with_own)
+            def _():
+                pltpu.make_async_copy(cot_recv.at[pl.ds(0, 3)], cot_recv.at[pl.ds(0, 3)], recv6.at[j]).wait()
+
+            @pl.when(jnp.logical_not(with_own))
+            def _():
+                pltpu.make_async_copy(cot_recv.at[pl.ds(0, 4)], cot_recv.at[pl.ds(0, 4)], recv6.at[j]).wait()
+
+        for i in range(many):
+            j = quad_at(s // 4, half * many + i, quads)
+            at = pl.ds(pl.multiple_of(j * 512, 512), 512)
+            right = one_right[:, at]
+            parts = []
+            for c in range(2):
+                row = jnp.concatenate([cot_recv[j * 4 + i, c : c + 1, :] for i in range(4)], axis=1)
+                parts.append(split(row))
+            scaled = [right * parts[c][part] for part in range(2) for c in range(2)]
+            total = total + dot(left_twice[:LANES, at], jnp.concatenate(scaled, axis=0), NT)
+        grids_ref[...] = total
+        return carry
+
+    grids_ref[...] = jnp.zeros_like(grids_ref)
+    lax.fori_loop(0, quads // many, scatter, 0)
+    grids = grids_ref[...]
     grids = grids[:, : 2 * LANES] + grids[:, 2 * LANES :]
     real, imag = grids[:, :LANES], grids[:, LANES:]
     real, imag = 0.5 * (real + real.T), 0.5 * (imag - imag.T)
@@ -426,23 +447,26 @@
             product = product[: 2 * LANES] + product[2 * LANES :]
             u_send[k, :, at] = jnp.sum(phased_sum[k, :, at] * product, axis=0, keepdims=True)
 
+    def send_gradient(peer):
+        pltpu.make_async_remote_copy(
+            src_ref=u_send.at[peer], dst_ref=u_recv.at[s], send_sem=send7, recv_sem=recv7,
+            device_id={"src": peer}, device_id_type=MESH,
+        ).start()
+
     def backward(step, carry):
         j = quad_at(s // 4, quads - 1 - step, quads)
         for i in range(4):
             pull_back(j * 4 + i)
         for i in range(4):
-            peer = j * 4 + i
-
-            @pl.when(peer != s)
-            def _():
-                pltpu.make_async_remote_copy(
-                    src_ref=u_send.at[peer], dst_ref=u_recv.at[s], send_sem=send7, recv_sem=recv7,
-                    device_id={"src": peer}, device_id_type=MESH,
-                ).start()
-
-        return carry
-
-    lax.fori_loop(0, quads, backward, 0)
+            send_gradient(j * 4 + i)
+        return carry
+
+    lax.fori_loop(0, quads - 1, backward, 0)
+    for step in (2, 1, 3):
+        pull_back(in_quad(s, step))
+    for step in (2, 1, 3):
+        send_gradient(in_quad(s, step))
+    pull_back(s)
     u_recv[s] = u_send[s]
     pltpu.make_async_copy(u_send.at[most], u_recv.at[most], recv7).wait()
     for i in range(ns):
@@ -504,20 +528,21 @@
         scratch_shapes=[
             (pltpu.SMEM if i == 3 else pltpu.VMEM)(value.shape, value.dtype) for i, value in enumerate(inputs)
         ] + [
-            pltpu.VMEM((ns, 4, slots), F32),
-            pltpu.VMEM((ns, 4, slots), F32),
+            pltpu.VMEM((ns, 12, LANES), F32),
+            pltpu.VMEM((ns, 12, LANES), F32),
             pltpu.VMEM((ns, 2 * LANES, slots), BF16),
             pltpu.VMEM((ns, 2 * LANES, slots), BF16),
             pltpu.VMEM((ns, 2 * LANES, slots), F32),
             pltpu.VMEM((2 * LANES, ns * LANES), BF16),
             pltpu.VMEM((LANES, ns * LANES), BF16),
-            pltpu.VMEM((LANES, LANES), BF16),
+            pltpu.VMEM((4 * LANES, LANES), BF16),
             pltpu.VMEM((2 * LANES, slots), BF16),
             pltpu.VMEM((2 * LANES, slots), BF16),
             pltpu.VMEM((2 * LANES, slots), BF16),
             pltpu.VMEM((2 * LANES, slots), BF16),
             pltpu.VMEM((2 * LANES, 2 * LANES), F32),
             pltpu.VMEM((2 * LANES, 2 * LANES), F32),
+            pltpu.VMEM((LANES, 4 * LANES), F32),
             pltpu.VMEM((ns, 2, LANES), F32),
             pltpu.VMEM((nch, 2, LANES), F32),
             pltpu.VMEM((2 * nch, LANES), F32),

time: 62.9 us -> 60.3 us (0.959)
  Pallas kernels: 60.9 us -> 58.3 us
    pallas_call x1, Pallas kernels: 60.9 us -> 58.3 us  [body(): pl.pallas_call(functools.partial(kernel, ns, nf, min(3, nf - 1)), out_sha...]
where the time goes in v5:
time: 60.3 us; the launch traced here: 60.2 us
  Pallas kernels  58.3 us (97%)
  other arithmetic  1.23 us (2%)
  between operations  0.67 us (1%)
    pallas_call x1, Pallas kernels, body(): pl.pallas_call(functools.partial(kernel, ns, nf, min(3, nf - 1)), out_sha...  58.3 us
    div x2, other arithmetic, body(): return (total[0] / flux, 2.0 * gradient / beam)  1.23 us

profile of v5, /device:TPU:1, one launch (start us, length us, event | category | flops | bytes accessed | tf_op | source)
XLA Modules:
  0.0 60.2 jit_solution(5476378207385010466)
XLA Ops:
  0.6 0.0 copy-start.1
  0.6 0.0 copy-start
  0.7 58.3 %shard_map.104 = (f32[32,512]{1,0:T(8,128)S(1)}, f32[1,512]{1,0:T(1,128)S(1)}) custom-call(f32[2,512]{1,0:T(2,128)} %dirs_hbm.1, f32[1,512]{1,0:T(1,128)} %bitcast.5, f32[32,512]{1,0:T(8,128)} %beam_hbm.1, s32[32]{0:T(128)} %counts_hbm.1, f32[3,128]{1,0:T(4,128)} %ant_hbm.1, s32[2,4096]{1,0:T(2,128)} %pairs_hbm.1, f32[2,16,256]{2,1,0:T(8,128)} %bitcast.6, ...), custom_call_target="tpu_custom_call" | custom-call | flops 8589934592 | bytes 4194304 | tf_op jit(solution)/shard_map/pallas_call | solution.py:520
  59.0 0.0 copy-done.1
  59.0 0.6 div.6
  59.6 0.0 copy-done
  59.6 0.6 %multiply_divide_fusion = f32[32,512]{1,0:T(8,128)} fusion(f32[32,512]{1,0:T(8,128)S(1)} %copy-done, f32[32,512]{1,0:T(8,128)S(1)} %get-tuple-element.5), kind=kLoop, calls=%fused_computation | loop fusion | flops 32768 | bytes 196608 | tf_op jit(solution)/shard_map/div | solution.py:571
Async XLA Ops:
  0.6 58.3 %copy-start.1 = (f32[512]{0:T(512)S(1)}, f32[512]{0:T(512)}, u32[]{:S(2)}) copy-start(f32[512]{0:T(512)} %param.10) | copy-start | bytes 6148
  0.6 58.9 %copy-start = (f32[32,512]{1,0:T(8,128)S(1)}, f32[32,512]{1,0:T(8,128)}, u32[]{:S(2)}) copy-start(f32[32,512]{1,0:T(8,128)} %beam_hbm.1) | copy-start | bytes 196612

commit v6 on v5

--- a/solution.py
+++ b/solution.py
@@ -73,7 +73,8 @@
 def quad_at(own, step, count):
     if count != 8:
         return lax.rem(own + step, count)
-    y = lax.rem(own // 2 + lax.rem(step, 4), 4)
+    place = lax.rem(step, 4)
+    y = lax.rem(own // 2 + place + place // 2 * (5 - 2 * place), 4)
     z = lax.rem(lax.rem(own, 2) + step // 4, 2)
     return y * 2 + z
 
@@ -104,8 +105,6 @@
             (tables_hbm, tables),
         ))
     ]
-    for copy in inputs:
-        copy.start()
     barrier = pltpu.get_barrier_semaphore()
 
     def greet(peer, group):
@@ -138,6 +137,8 @@
 
     lax.fori_loop(0, quads, greet_quad, 0)
     lax.fori_loop(1, nf, greet_freq, 0)
+    for copy in inputs:
+        copy.start()
     for copy in inputs[:8]:
         copy.wait()
 

time: 60.3 us -> 60.2 us (level)
  no operation moved by 1% of the time
where the time goes in v6:
time: 60.2 us; the launch traced here: 60.1 us
  Pallas kernels  58.2 us (97%)
  other arithmetic  1.23 us (2%)
  between operations  0.67 us (1%)
    pallas_call x1, Pallas kernels, body(): pl.pallas_call(functools.partial(kernel, ns, nf, min(3, nf - 1)), out_sha...  58.2 us
    div x2, other arithmetic, body(): return (total[0] / flux, 2.0 * gradient / beam)  1.23 us

profile of v6, /device:TPU:1, one launch (start us, length us, event | category | flops | bytes accessed | tf_op | source)
XLA Modules:
  0.0 60.1 jit_solution(14019225771027646139)
XLA Ops:
  0.6 0.0 copy-start.1
  0.6 0.0 copy-start
  0.7 58.2 %shard_map.104 = (f32[32,512]{1,0:T(8,128)S(1)}, f32[1,512]{1,0:T(1,128)S(1)}) custom-call(f32[2,512]{1,0:T(2,128)} %dirs_hbm.1, f32[1,512]{1,0:T(1,128)} %bitcast.5, f32[32,512]{1,0:T(8,128)} %beam_hbm.1, s32[32]{0:T(128)} %counts_hbm.1, f32[3,128]{1,0:T(4,128)} %ant_hbm.1, s32[2,4096]{1,0:T(2,128)} %pairs_hbm.1, f32[2,16,256]{2,1,0:T(8,128)} %bitcast.6, ...), custom_call_target="tpu_custom_call" | custom-call | flops 8589934592 | bytes 4194304 | tf_op jit(solution)/shard_map/pallas_call | solution.py:521
  58.9 0.0 copy-done.1
  58.9 0.6 div.6
  59.5 0.0 copy-done
  59.5 0.6 %multiply_divide_fusion = f32[32,512]{1,0:T(8,128)} fusion(f32[32,512]{1,0:T(8,128)S(1)} %copy-done, f32[32,512]{1,0:T(8,128)S(1)} %get-tuple-element.5), kind=kLoop, calls=%fused_computation | loop fusion | flops 32768 | bytes 196608 | tf_op jit(solution)/shard_map/div | solution.py:572
Async XLA Ops:
  0.6 58.2 %copy-start.1 = (f32[512]{0:T(512)S(1)}, f32[512]{0:T(512)}, u32[]{:S(2)}) copy-start(f32[512]{0:T(512)} %param.10) | copy-start | bytes 6148
  0.6 58.8 %copy-start = (f32[32,512]{1,0:T(8,128)S(1)}, f32[32,512]{1,0:T(8,128)}, u32[]{:S(2)}) copy-start(f32[32,512]{1,0:T(8,128)} %beam_hbm.1) | copy-start | bytes 196612

commit v7 on v6

--- a/solution.py
+++ b/solution.py
@@ -425,16 +425,16 @@
                 row = jnp.concatenate([cot_recv[j * 4 + i, c : c + 1, :] for i in range(4)], axis=1)
                 parts.append(split(row))
             scaled = [right * parts[c][part] for part in range(2) for c in range(2)]
-            total = total + dot(left_twice[:LANES, at], jnp.concatenate(scaled, axis=0), NT)
+            total = total + dot(jnp.concatenate(scaled, axis=0), left_twice[:LANES, at], NT)
         grids_ref[...] = total
         return carry
 
     grids_ref[...] = jnp.zeros_like(grids_ref)
     lax.fori_loop(0, quads // many, scatter, 0)
     grids = grids_ref[...]
-    grids = grids[:, : 2 * LANES] + grids[:, 2 * LANES :]
-    real, imag = grids[:, :LANES], grids[:, LANES:]
-    real, imag = 0.5 * (real + real.T), 0.5 * (imag - imag.T)
+    grids = grids[: 2 * LANES] + grids[2 * LANES :]
+    real, imag = grids[:LANES], grids[LANES:]
+    real, imag = 0.5 * (real + real.T), 0.5 * (imag.T - imag)
     matrix = jnp.concatenate(
         [jnp.concatenate([real, -imag], axis=1), jnp.concatenate([imag, real], axis=1)], axis=0
     )
@@ -543,7 +543,7 @@
             pltpu.VMEM((2 * LANES, slots), BF16),
             pltpu.VMEM((2 * LANES, 2 * LANES), F32),
             pltpu.VMEM((2 * LANES, 2 * LANES), F32),
-            pltpu.VMEM((LANES, 4 * LANES), F32),
+            pltpu.VMEM((4 * LANES, LANES), F32),
             pltpu.VMEM((ns, 2, LANES), F32),
             pltpu.VMEM((nch, 2, LANES), F32),
             pltpu.VMEM((2 * nch, LANES), F32),

time: 60.2 us -> 60 us (level)
  no operation moved by 1% of the time
where the time goes in v7:
time: 60 us; the launch traced here: 59.9 us
  Pallas kernels  58 us (97%)
  other arithmetic  1.23 us (2%)
  between operations  0.67 us (1%)
    pallas_call x1, Pallas kernels, body(): pl.pallas_call(functools.partial(kernel, ns, nf, min(3, nf - 1)), out_sha...  58 us
    div x2, other arithmetic, body(): return (total[0] / flux, 2.0 * gradient / beam)  1.23 us

profile of v7, /device:TPU:1, one launch (start us, length us, event | category | flops | bytes accessed | tf_op | source)
XLA Modules:
  0.0 59.9 jit_solution(7219793663543814950)
XLA Ops:
  0.6 0.0 copy-start.1
  0.6 0.0 copy-start
  0.7 58.0 %shard_map.104 = (f32[32,512]{1,0:T(8,128)S(1)}, f32[1,512]{1,0:T(1,128)S(1)}) custom-call(f32[2,512]{1,0:T(2,128)} %dirs_hbm.1, f32[1,512]{1,0:T(1,128)} %bitcast.5, f32[32,512]{1,0:T(8,128)} %beam_hbm.1, s32[32]{0:T(128)} %counts_hbm.1, f32[3,128]{1,0:T(4,128)} %ant_hbm.1, s32[2,4096]{1,0:T(2,128)} %pairs_hbm.1, f32[2,16,256]{2,1,0:T(8,128)} %bitcast.6, ...), custom_call_target="tpu_custom_call" | custom-call | flops 8589934592 | bytes 4194304 | tf_op jit(solution)/shard_map/pallas_call | solution.py:521
  58.6 0.0 copy-done.1
  58.7 0.6 div.6
  59.2 0.0 copy-done
  59.2 0.6 %multiply_divide_fusion = f32[32,512]{1,0:T(8,128)} fusion(f32[32,512]{1,0:T(8,128)S(1)} %copy-done, f32[32,512]{1,0:T(8,128)S(1)} %get-tuple-element.5), kind=kLoop, calls=%fused_computation | loop fusion | flops 32768 | bytes 196608 | tf_op jit(solution)/shard_map/div | solution.py:572
Async XLA Ops:
  0.6 58.0 %copy-start.1 = (f32[512]{0:T(512)S(1)}, f32[512]{0:T(512)}, u32[]{:S(2)}) copy-start(f32[512]{0:T(512)} %param.10) | copy-start | bytes 6148
  0.6 58.6 %copy-start = (f32[32,512]{1,0:T(8,128)S(1)}, f32[32,512]{1,0:T(8,128)}, u32[]{:S(2)}) copy-start(f32[32,512]{1,0:T(8,128)} %beam_hbm.1) | copy-start | bytes 196612
